TPU v7x, 512 devices: a whole 4x4x16 slice. The times are simulated.
512 devices in a mesh: phys: 2 (over x_hi), gx: 16 (over z), gy: 16 (over x_lo, y, core).
Axes of the slice: x: 4 (x_hi: 2, x_lo: 2; x = x_hi * 2 + x_lo), y: 4, z: 16, core: 2. Of those that a mesh axis runs over, the one named last changes fastest.
Arguments:
- models: float32 [2, 4, 1024, 2048], P('phys', None, 'gx', 'gy'), may hold values from -6 to 6
- channel_weight: float32 [2, 6], replicated, may hold values from 50 to 500
Outputs:
- gradient: float32 [2, 4, 1024, 2048], P('phys', None, 'gx', 'gy')
All inputs are finite; a program needn't handle non-finite values.
Results may differ from a plain program's by a relative error of at most 0.0001.
Values sent between devices are 32-bit elements; how exact they have to be, the bound alone decides.
No kernel may reach another device: no remote copies, remote signals or barrier semaphores. Data moves between devices by JAX's collectives and lax.ppermute only.
A program may use at most 64 MiB of HBM per device.

v0:
```python
import math

import jax
import jax.numpy as jnp
from jax import lax
from jax.sharding import PartitionSpec as P

gauss_total = sum((math.exp(-j * j / 50.0) for j in range(-15, 16)))


def extended(array, sides, width):
    for axis, dim in sides:
        peers, length = (lax.axis_size(axis), array.shape[dim])
        up = [(i, (i + 1) % peers) for i in range(peers - 1)]
        down = [(j, i) for i, j in up]
        last = lax.slice_in_dim(array, length - width, length, axis=dim)
        initial = lax.slice_in_dim(array, 0, width, axis=dim)
        before = lax.ppermute(last, axis, up)
        after = lax.ppermute(initial, axis, down)
        array = jnp.concatenate([before, array, after], axis=dim)
    return array


def from_partner(block, axis, stride):
    count = lax.axis_size(axis)
    route = []
    for low in range(count):
        high = low | 1 << stride
        if high != low and high < count:
            route += [(low, high), (high, low)]
    return lax.ppermute(block, axis, route)


def kernel_matrix(rows_n, cols_n, offset, dilation):
    row_index = lax.broadcasted_iota(jnp.int32, (rows_n, cols_n), 0)
    col_index = lax.broadcasted_iota(jnp.int32, (rows_n, cols_n), 1)
    distance = row_index - col_index + offset
    tap_index = distance // dilation
    on_tap = (distance == tap_index * dilation) & (jnp.abs(tap_index) <= 15)
    tap_float = tap_index.astype(jnp.float32)
    weights = jnp.exp(-tap_float * tap_float / 50.0) / gauss_total
    return jnp.where(on_tap, weights, 0.0)


def smooth_middle(values, dilation):
    lead, length, trail = values.shape
    highest = lax.Precision.HIGHEST
    if length <= 256:
        return jnp.einsum(
            "ij,ajb->aib", kernel_matrix(length, length, 0, dilation), values, precision=highest
        )
    block_count = length // 128
    blocks = values.reshape(lead, block_count, 128, trail)
    zero_block = jnp.zeros((lead, 1, 128, trail), values.dtype)
    after_blocks = jnp.concatenate([blocks[:, 1:], zero_block], 1)
    before_blocks = jnp.concatenate([zero_block, blocks[:, :-1]], 1)
    result = jnp.einsum(
        "ij,anjb->anib", kernel_matrix(128, 128, 0, dilation), blocks, precision=highest
    )
    result = result + jnp.einsum(
        "ij,anjb->anib", kernel_matrix(128, 128, -128, dilation), after_blocks, precision=highest
    )
    result = result + jnp.einsum(
        "ij,anjb->anib", kernel_matrix(128, 128, 128, dilation), before_blocks, precision=highest
    )
    return result.reshape(lead, length, trail)


def smooth_last(values, dilation):
    lead, trail, length = values.shape
    highest = lax.Precision.HIGHEST
    block_count = length // 128
    blocks = values.reshape(lead, trail, block_count, 128)
    zero_block = jnp.zeros((lead, trail, 1, 128), values.dtype)
    after_blocks = jnp.concatenate([blocks[:, :, 1:], zero_block], 2)
    before_blocks = jnp.concatenate([zero_block, blocks[:, :, :-1]], 2)
    result = jnp.einsum(
        "ajnk,ik->ajni", blocks, kernel_matrix(128, 128, 0, dilation), precision=highest
    )
    result = result + jnp.einsum(
        "ajnk,ik->ajni", after_blocks, kernel_matrix(128, 128, -128, dilation), precision=highest
    )
    result = result + jnp.einsum(
        "ajnk,ik->ajni", before_blocks, kernel_matrix(128, 128, 128, dilation), precision=highest
    )
    return result.reshape(lead, trail, length)


def smooth_rows(row_stack):
    row_count, x_cells, y_cells = row_stack.shape
    half_rows = row_count // 2
    depth_cells = row_count // 12
    z_rows = row_stack.reshape(12, depth_cells, x_cells * y_cells)
    z_done = jnp.concatenate([smooth_middle(z_rows[:6], 1), smooth_middle(z_rows[6:], 4)], 0)
    z_done = z_done.reshape(row_count, x_cells, y_cells)
    per_device = row_count // lax.axis_size("gx")
    dilation = jnp.where(lax.axis_index("gx") * per_device >= half_rows, 4, 1)
    x_done = lax.all_to_all(
        smooth_middle(
            lax.all_to_all(z_done, "gx", split_axis=0, concat_axis=1, tiled=True), dilation
        ),
        "gx",
        split_axis=1,
        concat_axis=0,
        tiled=True,
    )
    per_column = row_count // lax.axis_size("gy")
    dilation = jnp.where(lax.axis_index("gy") * per_column >= half_rows, 4, 1)
    return lax.all_to_all(
        smooth_last(
            lax.all_to_all(x_done, "gy", split_axis=0, concat_axis=2, tiled=True), dilation
        ),
        "gy",
        split_axis=2,
        concat_axis=0,
        tiled=True,
    )


def shards(models, channel_weight):
    model_field = models[0]
    depth_cells, x_cells, y_cells = model_field.shape
    padded = extended(model_field, (("gx", 1), ("gy", 2)), 1)
    z_padded = jnp.pad(model_field, ((1, 1), (0, 0), (0, 0)))
    slope_x = 0.5 * (padded[:, 2:, 1:-1] - padded[:, :-2, 1:-1])
    slope_y = 0.5 * (padded[:, 1:-1, 2:] - padded[:, 1:-1, :-2])
    slope_z = 0.5 * (z_padded[2:] - z_padded[:-2])
    tensor = jnp.stack(
        [
            slope_x * slope_x,
            slope_y * slope_y,
            slope_z * slope_z,
            slope_x * slope_y,
            slope_x * slope_z,
            slope_y * slope_z,
        ],
        0,
    )
    row_stack = jnp.concatenate([tensor, tensor], 0).reshape(12 * depth_cells, x_cells, y_cells)
    smoothed = smooth_rows(row_stack)
    partner_part = from_partner(smoothed, "phys", 0)
    weights = jnp.repeat(channel_weight.reshape(12), depth_cells)[:, None, None]
    adjoint = smooth_rows((smoothed - partner_part) * weights)
    half_rows = 6 * depth_cells
    combined = (adjoint[:half_rows] + adjoint[half_rows:]).reshape(6, depth_cells, x_cells, y_cells)
    q_x = 2.0 * combined[0] * slope_x + combined[3] * slope_y + combined[4] * slope_z
    q_y = 2.0 * combined[1] * slope_y + combined[3] * slope_x + combined[5] * slope_z
    q_z = 2.0 * combined[2] * slope_z + combined[4] * slope_x + combined[5] * slope_y
    lateral = extended(jnp.stack([q_x, q_y], 0), (("gx", 2), ("gy", 3)), 1)
    pad_z = jnp.pad(q_z, ((1, 1), (0, 0), (0, 0)))
    result = 0.5 * (lateral[0, :, :-2, 1:-1] - lateral[0, :, 2:, 1:-1])
    result = result + 0.5 * (lateral[1, :, 1:-1, :-2] - lateral[1, :, 1:-1, 2:])
    result = result + 0.5 * (pad_z[:-2] - pad_z[2:])
    return result[None]


def solution(mesh):
    in_specs = (P("phys", None, "gx", "gy"), P())
    out_specs = P("phys", None, "gx", "gy")
    return jax.shard_map(shards, mesh=mesh, in_specs=in_specs, out_specs=out_specs, check_vma=False)
```

profile of v0, /device:TPU:25, one launch (start us, length us, event | category | flops | bytes accessed | tf_op | source)
XLA Modules:
  0.0 646.8 jit_solution(4827848419836089784)
XLA Ops:
  0.0 0.8 fusion.375
  0.8 1.3 collective-permute-start
  2.1 4.2 collective-permute-start.1
  7.0 0.9 pad_maximum_fusion.3
  8.0 3.5 collective-permute-start.2
  11.6 4.1 collective-permute-start.3
  15.7 0.9 collective-permute-done.2
  16.6 1.2 collective-permute-done.3
  17.8 1.3 fusion.367
  19.7 1.5 convolution_bitcast_fusion.2
  21.2 1.5 convolution_bitcast_fusion.3
  23.0 2.3 reshape.70
  25.3 16.5 %all-to-all-start = ((f32[48,64,128]{2,1,0:T(8,128)}), f32[48,64,128]{2,1,0:T(8,128)S(1)}, u32[]{:S(2)}, u32[]{:S(2)}) async-start(f32[48,64,128]{2,1,0:T(8,128)} %reshape.70), calls=%async_computation | async-start | bytes 3145728 | tf_op jit(solution)/shard_map/all_to_all | solution.py:100
  41.8 68.9 %all-to-all-done = f32[48,64,128]{2,1,0:T(8,128)S(1)} async-done(((f32[48,64,128]{2,1,0:T(8,128)}), f32[48,64,128]{2,1,0:T(8,128)S(1)}, u32[]{:S(2)}, u32[]{:S(2)}) %all-to-all-start) | async-done | bytes 1572896 | tf_op jit(solution)/shard_map/all_to_all | solution.py:100
  110.8 2.0 fusion.16
  112.8 2.2 fusion.102
  115.0 2.3 add_add_fusion.3
  117.4 1.1 copy.22
  118.4 101.6 %all_to_all.129 = f32[3,1024,128]{2,0,1:T(4,128)S(1)} all-to-all(f32[3,1024,128]{2,0,1:T(4,128)S(1)} %copy.22), channel_id=1, replica_groups=mesh['phys'=2,'gx'=16,'gy'=16] {'gx'}, dimensions={1} | all-to-all | bytes 3145728 | tf_op jit(solution)/shard_map/all_to_all | solution.py:98
  220.2 1.4 copy.24
  221.5 12.1 %all-to-all-start.2 = ((f32[48,64,128]{2,1,0:T(8,128)}), f32[48,64,128]{2,1,0:T(8,128)S(1)}, u32[]{:S(2)}, u32[]{:S(2)}) async-start(f32[48,64,128]{2,1,0:T(8,128)} %bitcast.19), calls=%async_computation.2 | async-start | bytes 3145728 | tf_op jit(solution)/shard_map/all_to_all | solution.py:111
  233.6 22.0 %all-to-all-done.2 = f32[48,64,128]{2,1,0:T(8,128)S(1)} async-done(((f32[48,64,128]{2,1,0:T(8,128)}), f32[48,64,128]{2,1,0:T(8,128)S(1)}, u32[]{:S(2)}, u32[]{:S(2)}) %all-to-all-start.2) | async-done | bytes 1572896 | tf_op jit(solution)/shard_map/all_to_all | solution.py:111
  255.7 0.9 copy.48
  256.8 2.9 fusion.98
  259.7 2.1 fusion.4
  261.9 2.1 add_add_fusion.2
  264.0 2.7 copy.41
  266.7 5.4 reshape.87
  272.1 24.6 %all_to_all.130 = f32[16,1,24576]{2,1,0:T(1,128)S(1)} all-to-all(f32[16,1,24576]{2,1,0:T(1,128)S(1)} %reshape.87), channel_id=1, replica_groups=mesh['phys'=2,'gx'=16,'gy'=16] {'gy'}, dimensions={0} | all-to-all | bytes 3145728 | tf_op jit(solution)/shard_map/all_to_all | solution.py:109
  297.2 4.4 reduce
  301.7 3.7 reshape.88
  305.4 3.3 copy.27
  308.7 4.6 collective-permute-start.4
  314.0 0.7 broadcast_in_dim.30
  315.4 32.5 %collective-permute-done.4 = f32[48,64,128]{2,1,0:T(8,128)S(1)} collective-permute-done((f32[48,64,128]{2,1,0:T(8,128)S(1)}, f32[48,64,128]{2,1,0:T(8,128)S(1)}, u32[]{:S(2)}, u32[]{:S(2)}) %collective-permute-start.4) | collective-permute-done | bytes 1572896 | tf_op jit(solution)/shard_map/ppermute | solution.py:31
  347.9 0.9 subtract_multiply_fusion
  349.2 1.5 convolution_bitcast_fusion
  351.0 1.5 convolution_bitcast_fusion.1
  352.9 1.1 reshape.75
  354.0 73.7 %all_to_all.131 = f32[48,64,128]{2,1,0:T(8,128)S(1)} all-to-all(f32[48,64,128]{2,1,0:T(8,128)S(1)} %reshape.75), channel_id=1, replica_groups=mesh['phys'=2,'gx'=16,'gy'=16] {'gx'}, dimensions={0} | all-to-all | bytes 3145728 | tf_op jit(solution)/shard_map/all_to_all | solution.py:100
  427.8 2.0 fusion.13
  429.8 2.2 fusion.100
  432.0 2.3 add_add_fusion.1
  434.4 1.1 copy.29
  435.5 102.2 %all_to_all.132 = f32[3,1024,128]{2,0,1:T(4,128)S(1)} all-to-all(f32[3,1024,128]{2,0,1:T(4,128)S(1)} %copy.29), channel_id=1, replica_groups=mesh['phys'=2,'gx'=16,'gy'=16] {'gx'}, dimensions={1} | all-to-all | bytes 3145728 | tf_op jit(solution)/shard_map/all_to_all | solution.py:98
  537.9 31.8 %all_to_all.133 = f32[48,64,128]{2,1,0:T(8,128)S(1)} all-to-all(f32[48,64,128]{2,1,0:T(8,128)S(1)} %bitcast.139), channel_id=1, replica_groups=mesh['phys'=2,'gx'=16,'gy'=16] {'gy'}, dimensions={0} | all-to-all | bytes 3145728 | tf_op jit(solution)/shard_map/all_to_all | solution.py:111
  569.7 0.9 copy.47
  570.6 2.9 fusion.96
  573.8 2.1 fusion
  575.9 2.2 add_add_fusion
  578.2 2.7 copy.42
  580.9 5.4 reshape.89
  586.3 24.9 %all_to_all.134 = f32[16,1,24576]{2,1,0:T(1,128)S(1)} all-to-all(f32[16,1,24576]{2,1,0:T(1,128)S(1)} %reshape.89), channel_id=1, replica_groups=mesh['phys'=2,'gx'=16,'gy'=16] {'gy'}, dimensions={0} | all-to-all | bytes 3145728 | tf_op jit(solution)/shard_map/all_to_all | solution.py:109
  611.2 4.4 reduce.1
  615.6 3.7 reshape.90
  619.3 2.8 slice_add_fusion
  622.9 2.7 collective-permute-start.5
  625.6 1.3 collective-permute-start.6
  627.0 3.0 collective-permute-done.6
  630.2 5.4 collective-permute-start.7
  635.6 1.9 collective-permute-start.8
  637.5 1.7 collective-permute-done.7
  639.2 6.5 %collective-permute-done.8 = f32[2,4,66,1]{3,2,1,0:T(8,128)S(1)} collective-permute-done((f32[2,4,66,1]{3,2,1,0:T(8,128)S(1)}, f32[2,4,66,1]{3,2,1,0:T(8,128)S(1)}, u32[]{:S(2)}, u32[]{:S(2)}) %collective-permute-start.8) | collective-permute-done | bytes 2144 | tf_op jit(solution)/shard_map/ppermute | solution.py:19
  645.7 0.8 fusion.23
  (42 shorter events, 6.7 us)
Async XLA Ops:
  0.0 19.1 %copy-start = (f32[1,4,64,128]{3,2,1,0:T(8,128)S(1)}, f32[1,4,64,128]{3,2,1,0:T(8,128)}, u32[]{:S(2)}) copy-start(f32[1,4,64,128]{3,2,1,0:T(8,128)} %param.2) | copy-start | bytes 393220
  0.8 5.5 collective-permute-start
  2.1 4.9 collective-permute-start.1
  8.0 8.6 %collective-permute-start.2 = (f32[4,66,1]{2,1,0:T(8,128)S(1)}, f32[4,66,1]{2,1,0:T(8,128)S(1)}, u32[]{:S(2)}, u32[]{:S(2)}) collective-permute-start(f32[4,66,1]{2,1,0:T(8,128)S(1)} %get-tuple-element.24), channel_id=1, source_target_pairs={{1,0},{2,1},{3,2},{4,3},{5,4},{6,5},{7,6},{8,7},{9,8},{10,9},{11,1... | collective-permute-start | bytes 3176 | tf_op jit(solution)/shard_map/ppermute | solution.py:19
  11.6 6.2 collective-permute-start.3
  25.3 85.4 %all-to-all-start = ((f32[48,64,128]{2,1,0:T(8,128)}), f32[48,64,128]{2,1,0:T(8,128)S(1)}, u32[]{:S(2)}, u32[]{:S(2)}) async-start(f32[48,64,128]{2,1,0:T(8,128)} %reshape.70), calls=%async_computation | async-start | bytes 3145728 | tf_op jit(solution)/shard_map/all_to_all | solution.py:100
  221.5 34.1 %all-to-all-start.2 = ((f32[48,64,128]{2,1,0:T(8,128)}), f32[48,64,128]{2,1,0:T(8,128)S(1)}, u32[]{:S(2)}, u32[]{:S(2)}) async-start(f32[48,64,128]{2,1,0:T(8,128)} %bitcast.19), calls=%async_computation.2 | async-start | bytes 3145728 | tf_op jit(solution)/shard_map/all_to_all | solution.py:111
  305.3 7.9 %copy-start.1 = (f32[2,6]{1,0:T(2,128)S(1)}, f32[2,6]{1,0:T(2,128)}, u32[]{:S(2)}) copy-start(f32[2,6]{1,0:T(2,128)} %param.3) | copy-start | bytes 148
  308.7 39.2 %collective-permute-start.4 = (f32[48,64,128]{2,1,0:T(8,128)S(1)}, f32[48,64,128]{2,1,0:T(8,128)S(1)}, u32[]{:S(2)}, u32[]{:S(2)}) collective-permute-start(f32[48,64,128]{2,1,0:T(8,128)S(1)} %bitcast.133), channel_id=1, source_target_pairs={{0,256},{256,0},{1,257},{257,1},{2,258},{258,2},{3,259},{259,3},{4... | collective-permute-start | bytes 4718600 | tf_op jit(solution)/shard_map/ppermute | solution.py:31
  622.9 4.0 collective-permute-start.5
  625.6 4.4 collective-permute-start.6
  630.2 9.1 %collective-permute-start.7 = (f32[2,4,66,1]{3,2,1,0:T(8,128)S(1)}, f32[2,4,66,1]{3,2,1,0:T(8,128)S(1)}, u32[]{:S(2)}, u32[]{:S(2)}) collective-permute-start(f32[2,4,66,1]{3,2,1,0:T(8,128)S(1)} %get-tuple-element.16), channel_id=1, source_target_pairs={{0,1},{1,2},{2,3},{3,4},{4,5},{5,6},{6,7},{7,8},{8,9},{9,10},{10,1... | collective-permute-start | bytes 6344 | tf_op jit(solution)/shard_map/ppermute | solution.py:18
  635.6 10.2 %collective-permute-start.8 = (f32[2,4,66,1]{3,2,1,0:T(8,128)S(1)}, f32[2,4,66,1]{3,2,1,0:T(8,128)S(1)}, u32[]{:S(2)}, u32[]{:S(2)}) collective-permute-start(f32[2,4,66,1]{3,2,1,0:T(8,128)S(1)} %get-tuple-element.17), channel_id=1, source_target_pairs={{1,0},{2,1},{3,2},{4,3},{5,4},{6,5},{7,6},{8,7},{9,8},{10,9},{11,1... | collective-permute-start | bytes 6344 | tf_op jit(solution)/shard_map/ppermute | solution.py:19
where the time goes:
time: 652 us; the launch traced here: 647 us
  blocking collectives  359 us (55%)
  waiting for transfers between devices  137 us (21%)
  starting transfers between devices  57.6 us (9%)
  local copies, waits for them, and re-layouts  42.1 us (6%)
  matrix products  33.3 us (5%)
  other arithmetic  16.6 us (3%)
    all_to_all x2, blocking collectives, smooth_rows(): lax.all_to_all(smooth_middle(lax.all_to_all(z_done, 'gx', split_axis=0, c...  204 us
    all_to_all x1, blocking collectives, smooth_rows(): lax.all_to_all(z_done, 'gx', split_axis=0, concat_axis=1, tiled=True)  73.7 us
    all_to_all x1, waiting for transfers between devices, smooth_rows(): lax.all_to_all(z_done, 'gx', split_axis=0, concat_axis=1, tiled=True)  68.9 us
    all_to_all x2, blocking collectives, smooth_rows(): lax.all_to_all(smooth_last(lax.all_to_all(x_done, 'gy', split_axis=0, con...  49.4 us
    ppermute x1, waiting for transfers between devices, from_partner(): return lax.ppermute(block, axis, route)  32.5 us
    all_to_all x1, blocking collectives, smooth_rows(): lax.all_to_all(x_done, 'gy', split_axis=0, concat_axis=2, tiled=True)  31.8 us
    all_to_all x1, waiting for transfers between devices, smooth_rows(): lax.all_to_all(x_done, 'gy', split_axis=0, concat_axis=2, tiled=True)  22 us
    unnamed x13, local copies, waits for them, and re-layouts  18.4 us
  transfers between devices with their start and end apart: 11, of which 9 were waited for; matrix products, arithmetic and copies ran while one was open for 0% of the time, Pallas kernels for 0%

commit v1 on v0

v1 whole, which is shorter than its diff:
```python
import math

import jax
import jax.numpy as jnp
import ml_dtypes
import numpy as np
from jax import lax
from jax.experimental import pallas as pl
from jax.experimental.pallas import tpu as pltpu
from jax.sharding import PartitionSpec as P

DILATIONS = (1, 4)
TAPS = 15
LANES = 128
ROWS = 80
KEPT = 72


def taps():
    weights = np.array([math.exp(-k * k / 50.0) for k in range(-TAPS, TAPS + 1)])
    return weights / weights.sum()


def squared(length, dilation):
    matrix = np.zeros((length, length))
    for k, weight in zip(range(-TAPS, TAPS + 1), taps()):
        matrix += weight * np.eye(length, k=dilation * k)
    return matrix @ matrix


def window(matrix, row_ids, col_ids):
    count = matrix.shape[0]
    row_ok = (row_ids >= 0) & (row_ids < count)
    col_ok = (col_ids >= 0) & (col_ids < count)
    picked = matrix[np.clip(row_ids, 0, count - 1)][:, np.clip(col_ids, 0, count - 1)]
    return picked * row_ok[:, None] * col_ok[None, :]


def chosen(tables, index):
    distinct, place = np.unique(tables, axis=0, return_inverse=True)
    high = distinct.astype(np.float32).astype(ml_dtypes.bfloat16)
    low = (distinct - high.astype(np.float64)).astype(np.float32).astype(ml_dtypes.bfloat16)
    which = jnp.asarray(place.reshape(-1).astype(np.int32))[index]
    return [lax.dynamic_index_in_dim(jnp.asarray(t), which, 0, False) for t in (high, low)]


def split_f32(value):
    high = value.astype(jnp.bfloat16)
    low = (value - high.astype(jnp.float32)).astype(jnp.bfloat16)
    return high, low


def off_grid(count):
    return np.full(count, -1)


def x_tables(peers, block):
    tables = []
    matrices = [squared(peers * block, d) for d in DILATIONS]
    for i in range(peers):
        start = i * block
        out_ids = np.concatenate(
            [
                np.arange(start, start + block + 1),
                off_grid(KEPT - block - 2),
                [start - 1],
                off_grid(ROWS - KEPT),
            ]
        )
        in_ids = np.arange(start - 2 * block, start + 3 * block)
        tables.append(np.concatenate([window(m, out_ids, in_ids) for m in matrices], 0))
    return np.stack(tables)


def y_tables(peers, block):
    tables = []
    fine, coarse = [squared(peers * block, d) for d in DILATIONS]
    for i in range(peers):
        start = i * block
        own = np.arange(start, start + block)
        left, right = own - block, own + block
        edge = np.concatenate([right[: block // 2], left[block // 2 :]])
        out_ids = np.concatenate(
            [own, [start + block], off_grid(block - 2), [start - 1]]
        )
        wide = np.concatenate([left, own, right])
        near = np.concatenate([own, edge])
        tables.append(
            np.concatenate(
                [window(coarse, out_ids, wide).T, window(fine, out_ids, near).T], 0
            )
        )
    return np.stack(tables)


def lane_index(shape):
    return lax.broadcasted_iota(jnp.int32, shape, len(shape) - 1)


def pack_kernel(ext_ref, left_ref, right_ref, out_ref):
    block = out_ref.shape[1] - 8
    start = 2 * block
    for z in range(out_ref.shape[0]):
        for column in range(2):
            def rows(at, count):
                if column == 0:
                    return ext_ref[z, at : at + count, :]
                l = left_ref[z, at : at + count, :]
                r = right_ref[z, at : at + count, :]
                return jnp.where(lane_index(l.shape) < LANES // 2, r, l)

            after, before = rows(start + block, 8), rows(start - 8, 8)
            sub = lax.broadcasted_iota(jnp.int32, after.shape, 0)
            lanes = slice(column * LANES, (column + 1) * LANES)
            out_ref[z, 0:block, lanes] = rows(start, block)
            out_ref[z, block : block + 8, lanes] = jnp.where(sub < 4, after, before)


def smooth_kernel(
    depth_w, weight_ref, ext_ref, left_ref, right_ref, xh_ref, xl_ref, yh_ref, yl_ref,
    out_ref, slope_ref, near_ref, high_ref, low_ref,
):
    depth, rows, _ = ext_ref.shape
    blocks = (left_ref, ext_ref, right_ref)
    chunk = 32
    centre = float(depth_w[1][0][0])

    x_both = jnp.concatenate([xh_ref[...], xl_ref[...]], 0)
    x_high = xh_ref[...]
    for pair in range(depth // 2):
        for k in range(2):
            z = 2 * pair + k
            for b in range(3):
                lanes = slice((3 * k + b) * LANES, (3 * k + b + 1) * LANES)
                for r in range(0, rows, chunk):
                    at = slice(r, r + chunk)
                    mid = blocks[b][z, at, :]
                    if r == 0:
                        before = jnp.concatenate([mid[:1], mid[:-1]], 0)
                    else:
                        before = blocks[b][z, r - 1 : r + chunk - 1, :]
                    if r + chunk == rows:
                        after = jnp.concatenate([mid[1:], mid[-1:]], 0)
                    else:
                        after = blocks[b][z, r + 1 : r + chunk + 1, :]
                    slope_ref[0, at, lanes] = 0.5 * (after - before)
                    lane = lane_index(mid.shape)
                    prev, nxt = pltpu.roll(mid, 1, 1), pltpu.roll(mid, LANES - 1, 1)
                    if b > 0:
                        prev = jnp.where(lane == 0, pltpu.roll(blocks[b - 1][z, at, :], 1, 1), prev)
                    if b < 2:
                        nxt = jnp.where(
                            lane == LANES - 1, pltpu.roll(blocks[b + 1][z, at, :], LANES - 1, 1), nxt
                        )
                    slope_ref[1, at, lanes] = 0.5 * (nxt - prev)
                    above = blocks[b][z + 1, at, :] if z + 1 < depth else jnp.zeros_like(mid)
                    below = blocks[b][z - 1, at, :] if z > 0 else jnp.zeros_like(mid)
                    slope_ref[2, at, lanes] = 0.5 * (above - below)
        for c, (i, j) in enumerate(((0, 0), (1, 1), (2, 2), (0, 1), (0, 2), (1, 2))):
            high, low = split_f32(slope_ref[i] * slope_ref[j])
            first = jnp.dot(x_both, high, preferred_element_type=jnp.float32)
            second = jnp.dot(x_high, low, preferred_element_type=jnp.float32)
            done = first[: 2 * ROWS] + first[2 * ROWS :] + second
            fine, coarse = done[:ROWS], done[ROWS:]
            scale = weight_ref[1, c] * centre
            for k in range(2):
                z = 2 * pair + k
                at = slice((c * depth + z) * ROWS, (c * depth + z + 1) * ROWS)
                wide = coarse[:, 3 * k * LANES : 3 * (k + 1) * LANES] * scale
                high_ref[at, : 3 * LANES], low_ref[at, : 3 * LANES] = split_f32(wide)
                l, o, r = [
                    fine[:, (3 * k + b) * LANES : (3 * k + b + 1) * LANES] for b in range(3)
                ]
                near_ref[c, z, :, :LANES] = o
                near_ref[c, z, :, LANES:] = jnp.where(lane_index(l.shape) < LANES // 2, r, l)
    for c in range(6):
        for z in range(depth):
            mixed = near_ref[c, 0] * (weight_ref[0, c] * float(depth_w[0][z][0]))
            for k in range(1, depth):
                mixed = mixed + near_ref[c, k] * (weight_ref[0, c] * float(depth_w[0][z][k]))
            at = slice((c * depth + z) * ROWS, (c * depth + z + 1) * ROWS)
            high_ref[at, 3 * LANES :], low_ref[at, 3 * LANES :] = split_f32(mixed)
    for c in range(6):
        at = slice(c * depth * ROWS, (c + 1) * depth * ROWS)
        high, low = high_ref[at, :], low_ref[at, :]
        done = jnp.dot(high, yh_ref[...], preferred_element_type=jnp.float32)
        done = done + jnp.dot(low, yh_ref[...], preferred_element_type=jnp.float32)
        done = done + jnp.dot(high, yl_ref[...], preferred_element_type=jnp.float32)
        for z in range(depth):
            out_ref[c, z] = done[z * ROWS : z * ROWS + KEPT]


def gradient_kernel(adj_ref, mine_ref, other_ref, own_ref, send_ref):
    depth, rows, cols = mine_ref.shape
    block = own_ref.shape[1]
    for model, result, sign in ((mine_ref, own_ref, 0.5), (other_ref, send_ref, -0.5)):
        q_z = []
        total = []
        for z in range(depth):
            m = model[z]
            s_x = 0.5 * (pltpu.roll(m, rows - 1, 0) - pltpu.roll(m, 1, 0))
            s_y = 0.5 * (pltpu.roll(m, cols - 1, 1) - pltpu.roll(m, 1, 1))
            above = model[z + 1] if z + 1 < depth else jnp.zeros_like(m)
            below = model[z - 1] if z > 0 else jnp.zeros_like(m)
            s_z = 0.5 * (above - below)
            a = [adj_ref[c, z] for c in range(6)]
            q_x = 2.0 * a[0] * s_x + a[3] * s_y + a[4] * s_z
            q_y = 2.0 * a[1] * s_y + a[3] * s_x + a[5] * s_z
            q_z.append((2.0 * a[2] * s_z + a[4] * s_x + a[5] * s_y)[:block, :LANES])
            lateral = pltpu.roll(q_x, 1, 0) - pltpu.roll(q_x, rows - 1, 0)
            lateral = lateral + pltpu.roll(q_y, 1, 1) - pltpu.roll(q_y, cols - 1, 1)
            total.append(lateral[:block, :LANES])
        for z in range(depth):
            value = total[z]
            if z > 0:
                value = value + q_z[z - 1]
            if z + 1 < depth:
                value = value - q_z[z + 1]
            result[z] = sign * value


def shift(value, axis, step):
    peers = lax.axis_size(axis)
    route = [(i, i + step) for i in range(peers) if 0 <= i + step < peers]
    return lax.ppermute(value, axis, route)


def solution(mesh):
    x_peers, y_peers = mesh.shape["gx"], mesh.shape["gy"]

    def shards(models, channel_weight):
        field = models[0]
        depth, x_cells, y_cells = field.shape
        depth_w = [squared(depth, d).tolist() for d in DILATIONS]
        x_index, y_index = lax.axis_index("gx"), lax.axis_index("gy")
        x_high, x_low = chosen(x_tables(x_peers, x_cells), x_index)
        y_high, y_low = chosen(y_tables(y_peers, y_cells), y_index)
        near = [shift(field, "gx", 1), shift(field, "gx", -1)]
        far = [shift(field, "gx", 2), shift(field, "gx", -2)]
        ext = jnp.concatenate([far[0], near[0], field, near[1], far[1]], 1)
        left, right = shift(ext, "gy", 1), shift(ext, "gy", -1)
        vmem = pl.BlockSpec(memory_space=pltpu.VMEM)
        smem = pl.BlockSpec(memory_space=pltpu.SMEM)
        params = pltpu.CompilerParams(vmem_limit_bytes=48 * 1024 * 1024)
        f32 = jnp.float32
        mine = pl.pallas_call(
            pack_kernel,
            out_shape=jax.ShapeDtypeStruct((depth, KEPT, 2 * LANES), f32),
            in_specs=[vmem] * 3,
            out_specs=vmem,
            compiler_params=params,
        )(ext, left, right)
        other = lax.ppermute(mine, "phys", [(0, 1), (1, 0)])
        rows = 5 * x_cells
        adjoint = pl.pallas_call(
            lambda *refs: smooth_kernel(depth_w, *refs),
            out_shape=jax.ShapeDtypeStruct((6, depth, KEPT, 2 * LANES), f32),
            in_specs=[smem] + [vmem] * 7,
            out_specs=vmem,
            scratch_shapes=[
                pltpu.VMEM((3, rows, 6 * LANES), f32),
                pltpu.VMEM((6, depth, ROWS, 2 * LANES), f32),
                pltpu.VMEM((6 * depth * ROWS, 5 * LANES), jnp.bfloat16),
                pltpu.VMEM((6 * depth * ROWS, 5 * LANES), jnp.bfloat16),
            ],
            compiler_params=params,
            cost_estimate=pl.CostEstimate(
                flops=8 * 10**9, bytes_accessed=4 * 10**6, transcendentals=0
            ),
        )(channel_weight, ext, left, right, x_high, x_low, y_high, y_low)
        own, send = pl.pallas_call(
            gradient_kernel,
            out_shape=[jax.ShapeDtypeStruct(field.shape, f32)] * 2,
            in_specs=[vmem] * 3,
            out_specs=[vmem] * 2,
            compiler_params=params,
        )(adjoint, mine, other)
        got = lax.ppermute(send, "phys", [(0, 1), (1, 0)])
        return (own + got)[None]

    in_specs = (P("phys", None, "gx", "gy"), P())
    out_specs = P("phys", None, "gx", "gy")
    return jax.shard_map(shards, mesh=mesh, in_specs=in_specs, out_specs=out_specs, check_vma=False)
```

time: 652 us -> 65.5 us (0.10)
  the two profiles are of different devices: /device:TPU:25 before, /device:TPU:73 now
where the time goes in v1:
time: 65.5 us; the launch traced here: 65.1 us
  starting transfers between devices  29.7 us (45%)
  waiting for transfers between devices  15.2 us (23%)
  Pallas kernels  9.92 us (15%)
  local copies, waits for them, and re-layouts  5.63 us (9%)
  between operations  3.97 us (6%)
  other arithmetic  0.67 us (1%)
    ppermute x6, starting transfers between devices, shift(): return lax.ppermute(value, axis, route)  22 us
    ppermute x6, waiting for transfers between devices, shift(): return lax.ppermute(value, axis, route)  9.6 us
    pallas_call x1, Pallas kernels, shards(): pl.pallas_call(lambda *refs: smooth_kernel(depth_w, *refs), out_shape=jax...  8.63 us
    ppermute x1, waiting for transfers between devices, shards(): got = lax.ppermute(send, 'phys', [(0, 1), (1, 0)])  5.59 us
    ppermute x1, starting transfers between devices, shards(): other = lax.ppermute(mine, 'phys', [(0, 1), (1, 0)])  4.65 us
    ppermute x1, starting transfers between devices, shards(): got = lax.ppermute(send, 'phys', [(0, 1), (1, 0)])  3.03 us
    dynamic_slice x2, local copies, waits for them, and re-layouts, chosen(): which = jnp.asarray(place.reshape(-1).astype(np.int32))[index]  2.55 us
    squeeze x2, local copies, waits for them, and re-layouts, chosen(): lax.dynamic_index_in_dim(jnp.asarray(t), which, 0, False)  2.12 us
  transfers between devices with their start and end apart: 8, of which 5 were waited for; matrix products, arithmetic and copies ran while one was open for 9% of the time, Pallas kernels for 13%

profile of v1, /device:TPU:73, one launch (start us, length us, event | category | flops | bytes accessed | tf_op | source)
XLA Modules:
  0.0 65.1 jit_solution(9367443116417656801)
XLA Ops:
  0.0 6.1 %collective-permute-start = (f32[4,64,128]{2,1,0:T(8,128)}, f32[4,64,128]{2,1,0:T(8,128)S(1)}, u32[]{:S(2)}, u32[]{:S(2)}) collective-permute-start(f32[4,64,128]{2,1,0:T(8,128)} %bitcast.14), channel_id=1, source_target_pairs={{0,32},{16,48},{32,64},{48,80},{64,96},{80,112},{96,128},{112,144}... | collective-permute-start | bytes 393224 | tf_op jit(solution)/shard_map/ppermute | solution.py:225
  6.1 3.5 %collective-permute-start.1 = (f32[4,64,128]{2,1,0:T(8,128)}, f32[4,64,128]{2,1,0:T(8,128)S(1)}, u32[]{:S(2)}, u32[]{:S(2)}) collective-permute-start(f32[4,64,128]{2,1,0:T(8,128)} %bitcast.15), channel_id=1, source_target_pairs={{0,16},{16,32},{32,48},{48,64},{64,80},{80,96},{96,112},{112,128},... | collective-permute-start | bytes 393224 | tf_op jit(solution)/shard_map/ppermute | solution.py:225
  9.7 1.9 %collective-permute-start.2 = (f32[4,64,128]{2,1,0:T(8,128)}, f32[4,64,128]{2,1,0:T(8,128)S(1)}, u32[]{:S(2)}, u32[]{:S(2)}) collective-permute-start(f32[4,64,128]{2,1,0:T(8,128)} %bitcast.16), channel_id=1, source_target_pairs={{16,0},{32,16},{48,32},{64,48},{80,64},{96,80},{112,96},{128,112},... | collective-permute-start | bytes 393224 | tf_op jit(solution)/shard_map/ppermute | solution.py:225
  11.6 1.9 %collective-permute-start.3 = (f32[4,64,128]{2,1,0:T(8,128)}, f32[4,64,128]{2,1,0:T(8,128)S(1)}, u32[]{:S(2)}, u32[]{:S(2)}) collective-permute-start(f32[4,64,128]{2,1,0:T(8,128)} %bitcast.17), channel_id=1, source_target_pairs={{32,0},{48,16},{64,32},{80,48},{96,64},{112,80},{128,96},{144,112}... | collective-permute-start | bytes 393224 | tf_op jit(solution)/shard_map/ppermute | solution.py:225
  13.5 0.0 collective-permute-done
  13.6 0.8 %collective-permute-done.1 = f32[4,64,128]{2,1,0:T(8,128)S(1)} collective-permute-done((f32[4,64,128]{2,1,0:T(8,128)}, f32[4,64,128]{2,1,0:T(8,128)S(1)}, u32[]{:S(2)}, u32[]{:S(2)}) %collective-permute-start.1) | collective-permute-done | bytes 131104 | tf_op jit(solution)/shard_map/ppermute | solution.py:225
  14.4 0.9 %constant_dynamic-update-slice_fusion.2 = f32[4,320,128]{2,1,0:T(8,128)S(1)} fusion(f32[4,320,128]{2,1,0:T(8,128)S(1)} %constant_dynamic-update-slice_fusion.3, f32[1,4,64,128]{3,2,1,0:T(8,128)} %param.8), kind=kLoop, calls=%fused_computation.7 | loop fusion | bytes 262144
  15.3 0.5 collective-permute-done.2
  15.8 6.9 %collective-permute-done.3 = f32[4,64,128]{2,1,0:T(8,128)S(1)} collective-permute-done((f32[4,64,128]{2,1,0:T(8,128)}, f32[4,64,128]{2,1,0:T(8,128)S(1)}, u32[]{:S(2)}, u32[]{:S(2)}) %collective-permute-start.3) | collective-permute-done | bytes 131104 | tf_op jit(solution)/shard_map/ppermute | solution.py:225
  22.7 6.6 %collective-permute-start.4 = (f32[4,320,128]{2,1,0:T(8,128)S(1)}, f32[4,320,128]{2,1,0:T(8,128)S(1)}, u32[]{:S(2)}, u32[]{:S(2)}) collective-permute-start(f32[4,320,128]{2,1,0:T(8,128)S(1)} %constant_dynamic-update-slice_fusion.refs_1_.ext_ref), channel_id=1, source_target_pairs={{0,1},{1,2},{2,3},{3,4},{4,5},{5,6},{6,7},{7,8},{8,9},{9,10},{10,1... | collective-permute-start | bytes 1966088 | tf_op jit(solution)/shard_map/ppermute | solution.py:225
  29.3 1.9 %collective-permute-start.5 = (f32[4,320,128]{2,1,0:T(8,128)S(1)}, f32[4,320,128]{2,1,0:T(8,128)S(1)}, u32[]{:S(2)}, u32[]{:S(2)}) collective-permute-start(f32[4,320,128]{2,1,0:T(8,128)S(1)} %constant_dynamic-update-slice_fusion.refs_1_.ext_ref), channel_id=1, source_target_pairs={{1,0},{2,1},{3,2},{4,3},{5,4},{6,5},{7,6},{8,7},{9,8},{10,9},{11,1... | collective-permute-start | bytes 1966088 | tf_op jit(solution)/shard_map/ppermute | solution.py:225
  31.2 1.3 %dynamic_slice.23 = s32[1]{0:T(128)} dynamic-slice(s32[16]{0:T(128)} %constant.40.clone, s32[]{:T(128)S(6)} %select_n.18), dynamic_slice_sizes={1} | dynamic-slice | bytes 12 | tf_op jit(solution)/shard_map/dynamic_slice | solution.py:43
  33.8 1.2 %dynamic_slice.20 = s32[1]{0:T(128)} dynamic-slice(s32[16]{0:T(128)} %constant.37.clone, s32[]{:T(128)S(6)} %select_n.16), dynamic_slice_sizes={1} | dynamic-slice | bytes 12 | tf_op jit(solution)/shard_map/dynamic_slice | solution.py:43
  37.6 1.0 %dynamic-slice_bitcast_fusion.2 = (bf16[160,320]{1,0:T(8,128)(2,1)S(1)}, bf16[160,320]{1,0:T(8,128)(2,1)S(1)}) fusion(bf16[7,160,320]{2,1,0:T(8,128)(2,1)} %constant.39.clone, s32[]{:T(128)S(6)} %select_n.17, bf16[7,160,320]{2,1,0:T(8,128)(2,1)} %constant.38.clone), kind=kLoop, calls=%fused_computation.3 | loop fusion | bytes 409604 | tf_op jit(solution)/shard_map/jit(dynamic_index_in_dim)/squeeze | solution.py:44
  38.6 0.0 copy-start
  38.6 1.1 %dynamic-slice_bitcast_fusion = (bf16[640,256]{1,0:T(8,128)(2,1)S(1)}, bf16[640,256]{1,0:T(8,128)(2,1)S(1)}) fusion(bf16[5,640,256]{2,1,0:T(8,128)(2,1)} %constant.42.clone, s32[]{:T(128)S(6)} %select_n.19, bf16[5,640,256]{2,1,0:T(8,128)(2,1)} %constant.41.clone), kind=kLoop, calls=%fused_computation | loop fusion | bytes 1310724 | tf_op jit(solution)/shard_map/jit(dynamic_index_in_dim)/squeeze | solution.py:44
  39.7 0.0 collective-permute-done.4.refs_2_.left_ref
  39.7 1.5 %collective-permute-done.5.refs_3_.right_ref = f32[4,320,128]{2,1,0:T(8,128)S(1)} collective-permute-done((f32[4,320,128]{2,1,0:T(8,128)S(1)}, f32[4,320,128]{2,1,0:T(8,128)S(1)}, u32[]{:S(2)}, u32[]{:S(2)}) %collective-permute-start.5) | collective-permute-done | bytes 655392 | tf_op jit(solution)/shard_map/ppermute | solution.py:225
  41.2 4.7 %collective-permute-start.6 = (f32[4,72,256]{2,1,0:T(8,128)S(1)}, f32[4,72,256]{2,1,0:T(8,128)S(1)}, u32[]{:S(2)}, u32[]{:S(2)}) collective-permute-start(f32[4,72,256]{2,1,0:T(8,128)S(1)} %shard_map.83.mine_ref), channel_id=1, source_target_pairs={{0,256},{256,0},{1,257},{257,1},{2,258},{258,2},{3,259},{259,3},{4... | collective-permute-start | bytes 884744 | tf_op jit(solution)/shard_map/ppermute | solution.py:253
  45.9 0.0 copy-done
  45.9 8.6 %shard_map.82.adj_ref = f32[6,4,72,256]{3,2,1,0:T(8,128)S(1)} custom-call(f32[2,6]{1,0:T(2,128)S(1)} %copy-done, f32[4,320,128]{2,1,0:T(8,128)S(1)} %constant_dynamic-update-slice_fusion.refs_1_.ext_ref, f32[4,320,128]{2,1,0:T(8,128)S(1)} %collective-permute-done.4.refs_2_.left_ref, f32[4,320,128]{2,1,0:T(8,128)S(1)} %collective-permute-done.5.refs_3_.right_ref, ...), custom_call_target="tpu_custom_call" | custom-call | flops 8000000000 | bytes 4000000 | tf_op jit(solution)/shard_map/pallas_call | solution.py:255
  54.5 0.0 collective-permute-done.6.other_ref
  54.5 1.3 %shard_map.84 = (f32[4,64,128]{2,1,0:T(8,128)S(1)}, f32[4,64,128]{2,1,0:T(8,128)S(1)}) custom-call(f32[6,4,72,256]{3,2,1,0:T(8,128)S(1)} %shard_map.82.adj_ref, f32[4,72,256]{2,1,0:T(8,128)S(1)} %shard_map.83.mine_ref, f32[4,72,256]{2,1,0:T(8,128)S(1)} %collective-permute-done.6.other_ref), custom_call_target="tpu_custom_call" | custom-call | tf_op jit(solution)/shard_map/pallas_call | solution.py:271
  55.8 3.0 %collective-permute-start.7 = (f32[4,64,128]{2,1,0:T(8,128)S(1)}, f32[4,64,128]{2,1,0:T(8,128)S(1)}, u32[]{:S(2)}, u32[]{:S(2)}) collective-permute-start(f32[4,64,128]{2,1,0:T(8,128)S(1)} %get-tuple-element.8), channel_id=1, source_target_pairs={{0,256},{256,0},{1,257},{257,1},{2,258},{258,2},{3,259},{259,3},{4... | collective-permute-start | bytes 393224 | tf_op jit(solution)/shard_map/ppermute | solution.py:278
  58.8 5.6 %collective-permute-done.7 = f32[4,64,128]{2,1,0:T(8,128)S(1)} collective-permute-done((f32[4,64,128]{2,1,0:T(8,128)S(1)}, f32[4,64,128]{2,1,0:T(8,128)S(1)}, u32[]{:S(2)}, u32[]{:S(2)}) %collective-permute-start.7) | collective-permute-done | bytes 131104 | tf_op jit(solution)/shard_map/ppermute | solution.py:278
  64.4 0.7 %add_bitcast_fusion = f32[1,4,64,128]{3,2,1,0:T(8,128)} fusion(f32[4,64,128]{2,1,0:T(8,128)S(1)} %get-tuple-element.7, f32[4,64,128]{2,1,0:T(8,128)S(1)} %collective-permute-done.7), kind=kLoop, calls=%fused_computation.2 | loop fusion | flops 32768 | bytes 393216 | tf_op jit(solution)/shard_map/broadcast_in_dim | solution.py:279
  (5 shorter events, 0.1 us)
Async XLA Ops:
  0.0 13.5 %collective-permute-start = (f32[4,64,128]{2,1,0:T(8,128)}, f32[4,64,128]{2,1,0:T(8,128)S(1)}, u32[]{:S(2)}, u32[]{:S(2)}) collective-permute-start(f32[4,64,128]{2,1,0:T(8,128)} %bitcast.14), channel_id=1, source_target_pairs={{0,32},{16,48},{32,64},{48,80},{64,96},{80,112},{96,128},{112,144}... | collective-permute-start | bytes 393224 | tf_op jit(solution)/shard_map/ppermute | solution.py:225
  6.1 8.3 %collective-permute-start.1 = (f32[4,64,128]{2,1,0:T(8,128)}, f32[4,64,128]{2,1,0:T(8,128)S(1)}, u32[]{:S(2)}, u32[]{:S(2)}) collective-permute-start(f32[4,64,128]{2,1,0:T(8,128)} %bitcast.15), channel_id=1, source_target_pairs={{0,16},{16,32},{32,48},{48,64},{64,80},{80,96},{96,112},{112,128},... | collective-permute-start | bytes 393224 | tf_op jit(solution)/shard_map/ppermute | solution.py:225
  9.7 6.1 %collective-permute-start.2 = (f32[4,64,128]{2,1,0:T(8,128)}, f32[4,64,128]{2,1,0:T(8,128)S(1)}, u32[]{:S(2)}, u32[]{:S(2)}) collective-permute-start(f32[4,64,128]{2,1,0:T(8,128)} %bitcast.16), channel_id=1, source_target_pairs={{16,0},{32,16},{48,32},{64,48},{80,64},{96,80},{112,96},{128,112},... | collective-permute-start | bytes 393224 | tf_op jit(solution)/shard_map/ppermute | solution.py:225
  11.6 11.0 %collective-permute-start.3 = (f32[4,64,128]{2,1,0:T(8,128)}, f32[4,64,128]{2,1,0:T(8,128)S(1)}, u32[]{:S(2)}, u32[]{:S(2)}) collective-permute-start(f32[4,64,128]{2,1,0:T(8,128)} %bitcast.17), channel_id=1, source_target_pairs={{32,0},{48,16},{64,32},{80,48},{96,64},{112,80},{128,96},{144,112}... | collective-permute-start | bytes 393224 | tf_op jit(solution)/shard_map/ppermute | solution.py:225
  22.7 17.1 %collective-permute-start.4 = (f32[4,320,128]{2,1,0:T(8,128)S(1)}, f32[4,320,128]{2,1,0:T(8,128)S(1)}, u32[]{:S(2)}, u32[]{:S(2)}) collective-permute-start(f32[4,320,128]{2,1,0:T(8,128)S(1)} %constant_dynamic-update-slice_fusion.refs_1_.ext_ref), channel_id=1, source_target_pairs={{0,1},{1,2},{2,3},{3,4},{4,5},{5,6},{6,7},{7,8},{8,9},{9,10},{10,1... | collective-permute-start | bytes 1966088 | tf_op jit(solution)/shard_map/ppermute | solution.py:225
  29.3 11.9 %collective-permute-start.5 = (f32[4,320,128]{2,1,0:T(8,128)S(1)}, f32[4,320,128]{2,1,0:T(8,128)S(1)}, u32[]{:S(2)}, u32[]{:S(2)}) collective-permute-start(f32[4,320,128]{2,1,0:T(8,128)S(1)} %constant_dynamic-update-slice_fusion.refs_1_.ext_ref), channel_id=1, source_target_pairs={{1,0},{2,1},{3,2},{4,3},{5,4},{6,5},{7,6},{8,7},{9,8},{10,9},{11,1... | collective-permute-start | bytes 1966088 | tf_op jit(solution)/shard_map/ppermute | solution.py:225
  38.6 7.3 %copy-start = (f32[2,6]{1,0:T(2,128)S(1)}, f32[2,6]{1,0:T(2,128)}, u32[]{:S(2)}) copy-start(f32[2,6]{1,0:T(2,128)} %refs_0_.1) | copy-start | bytes 148
  41.2 13.3 %collective-permute-start.6 = (f32[4,72,256]{2,1,0:T(8,128)S(1)}, f32[4,72,256]{2,1,0:T(8,128)S(1)}, u32[]{:S(2)}, u32[]{:S(2)}) collective-permute-start(f32[4,72,256]{2,1,0:T(8,128)S(1)} %shard_map.83.mine_ref), channel_id=1, source_target_pairs={{0,256},{256,0},{1,257},{257,1},{2,258},{258,2},{3,259},{259,3},{4... | collective-permute-start | bytes 884744 | tf_op jit(solution)/shard_map/ppermute | solution.py:253
  55.8 8.6 %collective-permute-start.7 = (f32[4,64,128]{2,1,0:T(8,128)S(1)}, f32[4,64,128]{2,1,0:T(8,128)S(1)}, u32[]{:S(2)}, u32[]{:S(2)}) collective-permute-start(f32[4,64,128]{2,1,0:T(8,128)S(1)} %get-tuple-element.8), channel_id=1, source_target_pairs={{0,256},{256,0},{1,257},{257,1},{2,258},{258,2},{3,259},{259,3},{4... | collective-permute-start | bytes 393224 | tf_op jit(solution)/shard_map/ppermute | solution.py:278

commit v2 on v1

--- a/solution.py
+++ b/solution.py
@@ -36,12 +36,19 @@
     return picked * row_ok[:, None] * col_ok[None, :]
 
 
-def chosen(tables, index):
-    distinct, place = np.unique(tables, axis=0, return_inverse=True)
-    high = distinct.astype(np.float32).astype(ml_dtypes.bfloat16)
-    low = (distinct - high.astype(np.float64)).astype(np.float32).astype(ml_dtypes.bfloat16)
-    which = jnp.asarray(place.reshape(-1).astype(np.int32))[index]
-    return [lax.dynamic_index_in_dim(jnp.asarray(t), which, 0, False) for t in (high, low)]
+def stored(tables, edge):
+    count = tables.shape[0]
+    if count > 2 * edge + 1:
+        tables = np.concatenate([tables[: edge + 1], tables[count - edge :]], 0)
+    high = tables.astype(np.float32).astype(ml_dtypes.bfloat16)
+    low = (tables - high.astype(np.float64)).astype(np.float32).astype(ml_dtypes.bfloat16)
+    return jnp.asarray(np.stack([high, low], 1))
+
+
+def table_of(index, count, edge):
+    if count <= 2 * edge + 1:
+        return index
+    return jnp.minimum(index, edge) + jnp.maximum(index - (count - 1 - edge), 0)
 
 
 def split_f32(value):
@@ -97,36 +104,46 @@
     return lax.broadcasted_iota(jnp.int32, shape, len(shape) - 1)
 
 
-def pack_kernel(ext_ref, left_ref, right_ref, out_ref):
+def pack_kernel(near_ref, left_ref, right_ref, out_ref):
     block = out_ref.shape[1] - 8
-    start = 2 * block
     for z in range(out_ref.shape[0]):
         for column in range(2):
             def rows(at, count):
                 if column == 0:
-                    return ext_ref[z, at : at + count, :]
+                    return near_ref[z, at : at + count, :]
                 l = left_ref[z, at : at + count, :]
                 r = right_ref[z, at : at + count, :]
                 return jnp.where(lane_index(l.shape) < LANES // 2, r, l)
 
-            after, before = rows(start + block, 8), rows(start - 8, 8)
+            after, before = rows(2 * block, 8), rows(block - 8, 8)
             sub = lax.broadcasted_iota(jnp.int32, after.shape, 0)
             lanes = slice(column * LANES, (column + 1) * LANES)
-            out_ref[z, 0:block, lanes] = rows(start, block)
+            out_ref[z, 0:block, lanes] = rows(block, block)
             out_ref[z, block : block + 8, lanes] = jnp.where(sub < 4, after, before)
 
 
 def smooth_kernel(
-    depth_w, weight_ref, ext_ref, left_ref, right_ref, xh_ref, xl_ref, yh_ref, yl_ref,
-    out_ref, slope_ref, near_ref, high_ref, low_ref,
+    depth_w, counts, which_ref, weight_ref, *refs
 ):
-    depth, rows, _ = ext_ref.shape
-    blocks = (left_ref, ext_ref, right_ref)
+    inner_refs, outer_refs, refs = refs[:3], refs[3:6], refs[6:]
+    x_all, y_all, out_ref, slope_ref, near_ref, high_ref, low_ref, ext_ref, x_ref, y_ref, x_sem, y_sem = refs
+    blocks, depth, rows, _ = ext_ref.shape
     chunk = 32
+    x_copy = pltpu.make_async_copy(x_all.at[table_of(which_ref[0], counts[0], 2)], x_ref, x_sem)
+    y_copy = pltpu.make_async_copy(y_all.at[table_of(which_ref[1], counts[1], 1)], y_ref, y_sem)
+    x_copy.start()
+    y_copy.start()
+    side = rows // 5
+    for b in range(blocks):
+        for z in range(depth):
+            ext_ref[b, z, side : 4 * side] = inner_refs[b][z]
+            ext_ref[b, z, :side] = outer_refs[b][z, :side]
+            ext_ref[b, z, 4 * side :] = outer_refs[b][z, side:]
+    x_copy.wait()
     centre = float(depth_w[1][0][0])
 
-    x_both = jnp.concatenate([xh_ref[...], xl_ref[...]], 0)
-    x_high = xh_ref[...]
+    x_both = jnp.concatenate([x_ref[0], x_ref[1]], 0)
+    x_high = x_ref[0]
     for pair in range(depth // 2):
         for k in range(2):
             z = 2 * pair + k
@@ -134,27 +151,27 @@
                 lanes = slice((3 * k + b) * LANES, (3 * k + b + 1) * LANES)
                 for r in range(0, rows, chunk):
                     at = slice(r, r + chunk)
-                    mid = blocks[b][z, at, :]
+                    mid = ext_ref[b, z, at, :]
                     if r == 0:
                         before = jnp.concatenate([mid[:1], mid[:-1]], 0)
                     else:
-                        before = blocks[b][z, r - 1 : r + chunk - 1, :]
+                        before = ext_ref[b, z, r - 1 : r + chunk - 1, :]
                     if r + chunk == rows:
                         after = jnp.concatenate([mid[1:], mid[-1:]], 0)
                     else:
-                        after = blocks[b][z, r + 1 : r + chunk + 1, :]
+                        after = ext_ref[b, z, r + 1 : r + chunk + 1, :]
                     slope_ref[0, at, lanes] = 0.5 * (after - before)
                     lane = lane_index(mid.shape)
                     prev, nxt = pltpu.roll(mid, 1, 1), pltpu.roll(mid, LANES - 1, 1)
                     if b > 0:
-                        prev = jnp.where(lane == 0, pltpu.roll(blocks[b - 1][z, at, :], 1, 1), prev)
+                        prev = jnp.where(lane == 0, pltpu.roll(ext_ref[b - 1, z, at, :], 1, 1), prev)
                     if b < 2:
                         nxt = jnp.where(
-                            lane == LANES - 1, pltpu.roll(blocks[b + 1][z, at, :], LANES - 1, 1), nxt
+                            lane == LANES - 1, pltpu.roll(ext_ref[b + 1, z, at, :], LANES - 1, 1), nxt
                         )
                     slope_ref[1, at, lanes] = 0.5 * (nxt - prev)
-                    above = blocks[b][z + 1, at, :] if z + 1 < depth else jnp.zeros_like(mid)
-                    below = blocks[b][z - 1, at, :] if z > 0 else jnp.zeros_like(mid)
+                    above = ext_ref[b, z + 1, at, :] if z + 1 < depth else jnp.zeros_like(mid)
+                    below = ext_ref[b, z - 1, at, :] if z > 0 else jnp.zeros_like(mid)
                     slope_ref[2, at, lanes] = 0.5 * (above - below)
         for c, (i, j) in enumerate(((0, 0), (1, 1), (2, 2), (0, 1), (0, 2), (1, 2))):
             high, low = split_f32(slope_ref[i] * slope_ref[j])
@@ -180,12 +197,13 @@
                 mixed = mixed + near_ref[c, k] * (weight_ref[0, c] * float(depth_w[0][z][k]))
             at = slice((c * depth + z) * ROWS, (c * depth + z + 1) * ROWS)
             high_ref[at, 3 * LANES :], low_ref[at, 3 * LANES :] = split_f32(mixed)
+    y_copy.wait()
     for c in range(6):
         at = slice(c * depth * ROWS, (c + 1) * depth * ROWS)
         high, low = high_ref[at, :], low_ref[at, :]
-        done = jnp.dot(high, yh_ref[...], preferred_element_type=jnp.float32)
-        done = done + jnp.dot(low, yh_ref[...], preferred_element_type=jnp.float32)
-        done = done + jnp.dot(high, yl_ref[...], preferred_element_type=jnp.float32)
+        done = jnp.dot(high, y_ref[0], preferred_element_type=jnp.float32)
+        done = done + jnp.dot(low, y_ref[0], preferred_element_type=jnp.float32)
+        done = done + jnp.dot(high, y_ref[1], preferred_element_type=jnp.float32)
         for z in range(depth):
             out_ref[c, z] = done[z * ROWS : z * ROWS + KEPT]
 
@@ -233,12 +251,15 @@
         depth, x_cells, y_cells = field.shape
         depth_w = [squared(depth, d).tolist() for d in DILATIONS]
         x_index, y_index = lax.axis_index("gx"), lax.axis_index("gy")
-        x_high, x_low = chosen(x_tables(x_peers, x_cells), x_index)
-        y_high, y_low = chosen(y_tables(y_peers, y_cells), y_index)
+        x_all = stored(x_tables(x_peers, x_cells), 2)
+        y_all = stored(y_tables(y_peers, y_cells), 1)
+        which = jnp.stack([x_index, y_index])
         near = [shift(field, "gx", 1), shift(field, "gx", -1)]
         far = [shift(field, "gx", 2), shift(field, "gx", -2)]
-        ext = jnp.concatenate([far[0], near[0], field, near[1], far[1]], 1)
-        left, right = shift(ext, "gy", 1), shift(ext, "gy", -1)
+        inner = jnp.concatenate([near[0], field, near[1]], 1)
+        inner_sides = [shift(inner, "gy", 1), shift(inner, "gy", -1)]
+        outer = jnp.concatenate(far, 1)
+        outer_sides = [shift(outer, "gy", 1), shift(outer, "gy", -1)]
         vmem = pl.BlockSpec(memory_space=pltpu.VMEM)
         smem = pl.BlockSpec(memory_space=pltpu.SMEM)
         params = pltpu.CompilerParams(vmem_limit_bytes=48 * 1024 * 1024)
@@ -249,25 +270,33 @@
             in_specs=[vmem] * 3,
             out_specs=vmem,
             compiler_params=params,
-        )(ext, left, right)
+        )(inner, *inner_sides)
         other = lax.ppermute(mine, "phys", [(0, 1), (1, 0)])
         rows = 5 * x_cells
         adjoint = pl.pallas_call(
-            lambda *refs: smooth_kernel(depth_w, *refs),
+            lambda *refs: smooth_kernel(depth_w, (x_peers, y_peers), *refs),
             out_shape=jax.ShapeDtypeStruct((6, depth, KEPT, 2 * LANES), f32),
-            in_specs=[smem] + [vmem] * 7,
+            in_specs=[smem] * 2 + [vmem] * 6 + [pl.BlockSpec(memory_space=pl.ANY)] * 2,
             out_specs=vmem,
             scratch_shapes=[
                 pltpu.VMEM((3, rows, 6 * LANES), f32),
                 pltpu.VMEM((6, depth, ROWS, 2 * LANES), f32),
                 pltpu.VMEM((6 * depth * ROWS, 5 * LANES), jnp.bfloat16),
                 pltpu.VMEM((6 * depth * ROWS, 5 * LANES), jnp.bfloat16),
+                pltpu.VMEM((3, depth, rows, LANES), f32),
+                pltpu.VMEM(x_all.shape[1:], jnp.bfloat16),
+                pltpu.VMEM(y_all.shape[1:], jnp.bfloat16),
+                pltpu.SemaphoreType.DMA,
+                pltpu.SemaphoreType.DMA,
             ],
             compiler_params=params,
             cost_estimate=pl.CostEstimate(
                 flops=8 * 10**9, bytes_accessed=4 * 10**6, transcendentals=0
             ),
-        )(channel_weight, ext, left, right, x_high, x_low, y_high, y_low)
+        )(
+            which, channel_weight, inner_sides[0], inner, inner_sides[1],
+            outer_sides[0], outer, outer_sides[1], x_all, y_all,
+        )
         own, send = pl.pallas_call(
             gradient_kernel,
             out_shape=[jax.ShapeDtypeStruct(field.shape, f32)] * 2,

time: 65.5 us -> 59.2 us (0.904)
  the two profiles are of different devices: /device:TPU:73 before, /device:TPU:25 now
where the time goes in v2:
time: 59.2 us; the launch traced here: 58.1 us
  starting transfers between devices  32.3 us (55%)
  waiting for transfers between devices  13.4 us (23%)
  Pallas kernels  10.6 us (18%)
  other arithmetic  1.69 us (3%)
    ppermute x8, starting transfers between devices, shift(): return lax.ppermute(value, axis, route)  23.2 us
    ppermute x8, waiting for transfers between devices, shift(): return lax.ppermute(value, axis, route)  10.9 us
    pallas_call x1, Pallas kernels, shards(): pl.pallas_call(lambda *refs: smooth_kernel(depth_w, (x_peers, y_peers), *...  9.29 us
    ppermute x1, starting transfers between devices, shards(): got = lax.ppermute(send, 'phys', [(0, 1), (1, 0)])  4.79 us
    ppermute x1, starting transfers between devices, shards(): other = lax.ppermute(mine, 'phys', [(0, 1), (1, 0)])  4.36 us
    ppermute x1, waiting for transfers between devices, shards(): got = lax.ppermute(send, 'phys', [(0, 1), (1, 0)])  2.42 us
    pallas_call x1, Pallas kernels, shards(): pl.pallas_call(gradient_kernel, out_shape=[jax.ShapeDtypeStruct(field.sha...  1.26 us
  transfers between devices with their start and end apart: 10, of which 3 were waited for; matrix products, arithmetic and copies ran while one was open for 2% of the time, Pallas kernels for 16%

profile of v2, /device:TPU:25, one launch (start us, length us, event | category | flops | bytes accessed | tf_op | source)
XLA Modules:
  0.0 58.1 jit_solution(6610388930025362007)
XLA Ops:
  0.0 0.0 copy-start.1
  0.0 0.0 copy-start
  0.0 3.7 %collective-permute-start = (f32[4,64,128]{2,1,0:T(8,128)}, f32[4,64,128]{2,1,0:T(8,128)S(1)}, u32[]{:S(2)}, u32[]{:S(2)}) collective-permute-start(f32[4,64,128]{2,1,0:T(8,128)} %bitcast.5), channel_id=1, source_target_pairs={{0,16},{16,32},{32,48},{48,64},{64,80},{80,96},{96,112},{112,128},... | collective-permute-start | bytes 393224 | tf_op jit(solution)/shard_map/ppermute | solution.py:243
  3.7 1.3 %collective-permute-start.1 = (f32[4,64,128]{2,1,0:T(8,128)}, f32[4,64,128]{2,1,0:T(8,128)S(1)}, u32[]{:S(2)}, u32[]{:S(2)}) collective-permute-start(f32[4,64,128]{2,1,0:T(8,128)} %bitcast.6), channel_id=1, source_target_pairs={{16,0},{32,16},{48,32},{64,48},{80,64},{96,80},{112,96},{128,112},... | collective-permute-start | bytes 393224 | tf_op jit(solution)/shard_map/ppermute | solution.py:243
  5.0 5.5 %collective-permute-start.4 = (f32[4,64,128]{2,1,0:T(8,128)}, f32[4,64,128]{2,1,0:T(8,128)S(1)}, u32[]{:S(2)}, u32[]{:S(2)}) collective-permute-start(f32[4,64,128]{2,1,0:T(8,128)} %bitcast.7), channel_id=1, source_target_pairs={{0,32},{16,48},{32,64},{48,80},{64,96},{80,112},{96,128},{112,144}... | collective-permute-start | bytes 393224 | tf_op jit(solution)/shard_map/ppermute | solution.py:243
  10.5 1.3 %collective-permute-start.5 = (f32[4,64,128]{2,1,0:T(8,128)}, f32[4,64,128]{2,1,0:T(8,128)S(1)}, u32[]{:S(2)}, u32[]{:S(2)}) collective-permute-start(f32[4,64,128]{2,1,0:T(8,128)} %bitcast.8), channel_id=1, source_target_pairs={{32,0},{48,16},{64,32},{80,48},{96,64},{112,80},{128,96},{144,112}... | collective-permute-start | bytes 393224 | tf_op jit(solution)/shard_map/ppermute | solution.py:243
  11.8 0.0 collective-permute-done
  11.8 0.0 collective-permute-done.1
  11.8 0.9 %pad_maximum_fusion.refs_3_.near_ref = f32[4,192,128]{2,1,0:T(8,128)S(1)} fusion(f32[4,64,128]{2,1,0:T(8,128)S(1)} %collective-permute-done.1, f32[4,64,128]{2,1,0:T(8,128)} %bitcast.9, f32[4,64,128]{2,1,0:T(8,128)S(1)} %collective-permute-done), kind=kLoop, calls=%fused_computation | loop fusion | flops 196608 | bytes 786432 | tf_op jit(solution)/shard_map/concatenate | solution.py:259
  12.8 4.0 %collective-permute-start.2 = (f32[4,192,128]{2,1,0:T(8,128)S(1)}, f32[4,192,128]{2,1,0:T(8,128)S(1)}, u32[]{:S(2)}, u32[]{:S(2)}) collective-permute-start(f32[4,192,128]{2,1,0:T(8,128)S(1)} %pad_maximum_fusion.refs_3_.near_ref), channel_id=1, source_target_pairs={{0,1},{1,2},{2,3},{3,4},{4,5},{5,6},{6,7},{7,8},{8,9},{9,10},{10,1... | collective-permute-start | bytes 1179656 | tf_op jit(solution)/shard_map/ppermute | solution.py:243
  16.8 1.9 %collective-permute-start.3 = (f32[4,192,128]{2,1,0:T(8,128)S(1)}, f32[4,192,128]{2,1,0:T(8,128)S(1)}, u32[]{:S(2)}, u32[]{:S(2)}) collective-permute-start(f32[4,192,128]{2,1,0:T(8,128)S(1)} %pad_maximum_fusion.refs_3_.near_ref), channel_id=1, source_target_pairs={{1,0},{2,1},{3,2},{4,3},{5,4},{6,5},{7,6},{8,7},{9,8},{10,9},{11,1... | collective-permute-start | bytes 1179656 | tf_op jit(solution)/shard_map/ppermute | solution.py:243
  18.7 0.0 collective-permute-done.4
  18.7 5.5 %collective-permute-done.5 = f32[4,64,128]{2,1,0:T(8,128)S(1)} collective-permute-done((f32[4,64,128]{2,1,0:T(8,128)}, f32[4,64,128]{2,1,0:T(8,128)S(1)}, u32[]{:S(2)}, u32[]{:S(2)}) %collective-permute-start.5) | collective-permute-done | bytes 131104 | tf_op jit(solution)/shard_map/ppermute | solution.py:243
  24.2 3.6 %collective-permute-start.6 = (f32[4,128,128]{2,1,0:T(8,128)S(1)}, f32[4,128,128]{2,1,0:T(8,128)S(1)}, u32[]{:S(2)}, u32[]{:S(2)}) collective-permute-start(f32[4,128,128]{2,1,0:T(8,128)S(1)} %constant_dynamic-update-slice_fusion.refs_6_), channel_id=1, source_target_pairs={{0,1},{1,2},{2,3},{3,4},{4,5},{5,6},{6,7},{7,8},{8,9},{9,10},{10,1... | collective-permute-start | bytes 786440 | tf_op jit(solution)/shard_map/ppermute | solution.py:243
  27.8 1.9 %collective-permute-start.7 = (f32[4,128,128]{2,1,0:T(8,128)S(1)}, f32[4,128,128]{2,1,0:T(8,128)S(1)}, u32[]{:S(2)}, u32[]{:S(2)}) collective-permute-start(f32[4,128,128]{2,1,0:T(8,128)S(1)} %constant_dynamic-update-slice_fusion.refs_6_), channel_id=1, source_target_pairs={{1,0},{2,1},{3,2},{4,3},{5,4},{6,5},{7,6},{8,7},{9,8},{10,9},{11,1... | collective-permute-start | bytes 786440 | tf_op jit(solution)/shard_map/ppermute | solution.py:243
  29.7 0.1 pad_add_fusion.refs_0_
  29.8 0.0 collective-permute-done.2.refs_2_.left_ref
  29.8 0.0 collective-permute-done.3.refs_4_.right_ref
  29.8 4.4 %collective-permute-start.8 = (f32[4,72,256]{2,1,0:T(8,128)S(1)}, f32[4,72,256]{2,1,0:T(8,128)S(1)}, u32[]{:S(2)}, u32[]{:S(2)}) collective-permute-start(f32[4,72,256]{2,1,0:T(8,128)S(1)} %shard_map.47.mine_ref), channel_id=1, source_target_pairs={{0,256},{256,0},{1,257},{257,1},{2,258},{258,2},{3,259},{259,3},{4... | collective-permute-start | bytes 884744 | tf_op jit(solution)/shard_map/ppermute | solution.py:274
  34.2 0.0 collective-permute-done.6.refs_5_
  34.2 5.4 %collective-permute-done.7.refs_7_ = f32[4,128,128]{2,1,0:T(8,128)S(1)} collective-permute-done((f32[4,128,128]{2,1,0:T(8,128)S(1)}, f32[4,128,128]{2,1,0:T(8,128)S(1)}, u32[]{:S(2)}, u32[]{:S(2)}) %collective-permute-start.7) | collective-permute-done | bytes 262176 | tf_op jit(solution)/shard_map/ppermute | solution.py:243
  39.7 0.0 copy-done.1
  39.7 0.0 copy-done
  39.7 9.3 %shard_map.46.adj_ref = f32[6,4,72,256]{3,2,1,0:T(8,128)S(1)} custom-call(s32[2]{0:T(128)S(1)} %pad_add_fusion.refs_0_, f32[2,6]{1,0:T(2,128)S(1)} %copy-done, f32[4,192,128]{2,1,0:T(8,128)S(1)} %collective-permute-done.2.refs_2_.left_ref, f32[4,192,128]{2,1,0:T(8,128)S(1)} %pad_maximum_fusion.refs_3_.near_ref, ...), custom_call_target="tpu_custom_call" | custom-call | flops 8000000000 | bytes 4000000 | tf_op jit(solution)/shard_map/pallas_call | solution.py:276
  49.0 0.0 collective-permute-done.8.other_ref
  49.0 1.3 %shard_map.48 = (f32[4,64,128]{2,1,0:T(8,128)S(1)}, f32[4,64,128]{2,1,0:T(8,128)S(1)}) custom-call(f32[6,4,72,256]{3,2,1,0:T(8,128)S(1)} %shard_map.46.adj_ref, f32[4,72,256]{2,1,0:T(8,128)S(1)} %shard_map.47.mine_ref, f32[4,72,256]{2,1,0:T(8,128)S(1)} %collective-permute-done.8.other_ref), custom_call_target="tpu_custom_call" | custom-call | tf_op jit(solution)/shard_map/pallas_call | solution.py:300
  50.2 4.8 %collective-permute-start.9 = (f32[4,64,128]{2,1,0:T(8,128)S(1)}, f32[4,64,128]{2,1,0:T(8,128)S(1)}, u32[]{:S(2)}, u32[]{:S(2)}) collective-permute-start(f32[4,64,128]{2,1,0:T(8,128)S(1)} %get-tuple-element.8), channel_id=1, source_target_pairs={{0,256},{256,0},{1,257},{257,1},{2,258},{258,2},{3,259},{259,3},{4... | collective-permute-start | bytes 393224 | tf_op jit(solution)/shard_map/ppermute | solution.py:307
  55.0 2.4 %collective-permute-done.9 = f32[4,64,128]{2,1,0:T(8,128)S(1)} collective-permute-done((f32[4,64,128]{2,1,0:T(8,128)S(1)}, f32[4,64,128]{2,1,0:T(8,128)S(1)}, u32[]{:S(2)}, u32[]{:S(2)}) %collective-permute-start.9) | collective-permute-done | bytes 131104 | tf_op jit(solution)/shard_map/ppermute | solution.py:307
  57.5 0.7 %add_bitcast_fusion = f32[1,4,64,128]{3,2,1,0:T(8,128)} fusion(f32[4,64,128]{2,1,0:T(8,128)S(1)} %get-tuple-element.7, f32[4,64,128]{2,1,0:T(8,128)S(1)} %collective-permute-done.9), kind=kLoop, calls=%fused_computation.1 | loop fusion | flops 32768 | bytes 393216 | tf_op jit(solution)/shard_map/broadcast_in_dim | solution.py:308
  (3 shorter events, 0.0 us)
Async XLA Ops:
  0.0 39.7 %copy-start.1 = (bf16[5,2,160,320]{3,2,1,0:T(8,128)(2,1)S(1)}, bf16[5,2,160,320]{3,2,1,0:T(8,128)(2,1)}, u32[]{:S(2)}) copy-start(bf16[5,2,160,320]{3,2,1,0:T(8,128)(2,1)} %constant.11.clone.refs_8_) | copy-start | bytes 3072004
  0.0 39.7 %copy-start = (f32[2,6]{1,0:T(2,128)S(1)}, f32[2,6]{1,0:T(2,128)}, u32[]{:S(2)}) copy-start(f32[2,6]{1,0:T(2,128)} %refs_1_.1) | copy-start | bytes 148
  0.0 11.8 %collective-permute-start = (f32[4,64,128]{2,1,0:T(8,128)}, f32[4,64,128]{2,1,0:T(8,128)S(1)}, u32[]{:S(2)}, u32[]{:S(2)}) collective-permute-start(f32[4,64,128]{2,1,0:T(8,128)} %bitcast.5), channel_id=1, source_target_pairs={{0,16},{16,32},{32,48},{48,64},{64,80},{80,96},{96,112},{112,128},... | collective-permute-start | bytes 393224 | tf_op jit(solution)/shard_map/ppermute | solution.py:243
  3.7 8.1 %collective-permute-start.1 = (f32[4,64,128]{2,1,0:T(8,128)}, f32[4,64,128]{2,1,0:T(8,128)S(1)}, u32[]{:S(2)}, u32[]{:S(2)}) collective-permute-start(f32[4,64,128]{2,1,0:T(8,128)} %bitcast.6), channel_id=1, source_target_pairs={{16,0},{32,16},{48,32},{64,48},{80,64},{96,80},{112,96},{128,112},... | collective-permute-start | bytes 393224 | tf_op jit(solution)/shard_map/ppermute | solution.py:243
  5.0 13.7 %collective-permute-start.4 = (f32[4,64,128]{2,1,0:T(8,128)}, f32[4,64,128]{2,1,0:T(8,128)S(1)}, u32[]{:S(2)}, u32[]{:S(2)}) collective-permute-start(f32[4,64,128]{2,1,0:T(8,128)} %bitcast.7), channel_id=1, source_target_pairs={{0,32},{16,48},{32,64},{48,80},{64,96},{80,112},{96,128},{112,144}... | collective-permute-start | bytes 393224 | tf_op jit(solution)/shard_map/ppermute | solution.py:243
  10.5 13.7 %collective-permute-start.5 = (f32[4,64,128]{2,1,0:T(8,128)}, f32[4,64,128]{2,1,0:T(8,128)S(1)}, u32[]{:S(2)}, u32[]{:S(2)}) collective-permute-start(f32[4,64,128]{2,1,0:T(8,128)} %bitcast.8), channel_id=1, source_target_pairs={{32,0},{48,16},{64,32},{80,48},{96,64},{112,80},{128,96},{144,112}... | collective-permute-start | bytes 393224 | tf_op jit(solution)/shard_map/ppermute | solution.py:243
  12.8 17.0 %collective-permute-start.2 = (f32[4,192,128]{2,1,0:T(8,128)S(1)}, f32[4,192,128]{2,1,0:T(8,128)S(1)}, u32[]{:S(2)}, u32[]{:S(2)}) collective-permute-start(f32[4,192,128]{2,1,0:T(8,128)S(1)} %pad_maximum_fusion.refs_3_.near_ref), channel_id=1, source_target_pairs={{0,1},{1,2},{2,3},{3,4},{4,5},{5,6},{6,7},{7,8},{8,9},{9,10},{10,1... | collective-permute-start | bytes 1179656 | tf_op jit(solution)/shard_map/ppermute | solution.py:243
  16.8 13.0 %collective-permute-start.3 = (f32[4,192,128]{2,1,0:T(8,128)S(1)}, f32[4,192,128]{2,1,0:T(8,128)S(1)}, u32[]{:S(2)}, u32[]{:S(2)}) collective-permute-start(f32[4,192,128]{2,1,0:T(8,128)S(1)} %pad_maximum_fusion.refs_3_.near_ref), channel_id=1, source_target_pairs={{1,0},{2,1},{3,2},{4,3},{5,4},{6,5},{7,6},{8,7},{9,8},{10,9},{11,1... | collective-permute-start | bytes 1179656 | tf_op jit(solution)/shard_map/ppermute | solution.py:243
  24.2 10.0 %collective-permute-start.6 = (f32[4,128,128]{2,1,0:T(8,128)S(1)}, f32[4,128,128]{2,1,0:T(8,128)S(1)}, u32[]{:S(2)}, u32[]{:S(2)}) collective-permute-start(f32[4,128,128]{2,1,0:T(8,128)S(1)} %constant_dynamic-update-slice_fusion.refs_6_), channel_id=1, source_target_pairs={{0,1},{1,2},{2,3},{3,4},{4,5},{5,6},{6,7},{7,8},{8,9},{9,10},{10,1... | collective-permute-start | bytes 786440 | tf_op jit(solution)/shard_map/ppermute | solution.py:243
  27.8 11.9 %collective-permute-start.7 = (f32[4,128,128]{2,1,0:T(8,128)S(1)}, f32[4,128,128]{2,1,0:T(8,128)S(1)}, u32[]{:S(2)}, u32[]{:S(2)}) collective-permute-start(f32[4,128,128]{2,1,0:T(8,128)S(1)} %constant_dynamic-update-slice_fusion.refs_6_), channel_id=1, source_target_pairs={{1,0},{2,1},{3,2},{4,3},{5,4},{6,5},{7,6},{8,7},{9,8},{10,9},{11,1... | collective-permute-start | bytes 786440 | tf_op jit(solution)/shard_map/ppermute | solution.py:243
  29.8 19.1 %collective-permute-start.8 = (f32[4,72,256]{2,1,0:T(8,128)S(1)}, f32[4,72,256]{2,1,0:T(8,128)S(1)}, u32[]{:S(2)}, u32[]{:S(2)}) collective-permute-start(f32[4,72,256]{2,1,0:T(8,128)S(1)} %shard_map.47.mine_ref), channel_id=1, source_target_pairs={{0,256},{256,0},{1,257},{257,1},{2,258},{258,2},{3,259},{259,3},{4... | collective-permute-start | bytes 884744 | tf_op jit(solution)/shard_map/ppermute | solution.py:274
  50.2 7.2 %collective-permute-start.9 = (f32[4,64,128]{2,1,0:T(8,128)S(1)}, f32[4,64,128]{2,1,0:T(8,128)S(1)}, u32[]{:S(2)}, u32[]{:S(2)}) collective-permute-start(f32[4,64,128]{2,1,0:T(8,128)S(1)} %get-tuple-element.8), channel_id=1, source_target_pairs={{0,256},{256,0},{1,257},{257,1},{2,258},{258,2},{3,259},{259,3},{4... | collective-permute-start | bytes 393224 | tf_op jit(solution)/shard_map/ppermute | solution.py:307

commit v3 on v2

--- a/solution.py
+++ b/solution.py
@@ -12,8 +12,7 @@
 DILATIONS = (1, 4)
 TAPS = 15
 LANES = 128
-ROWS = 80
-KEPT = 72
+ROWS = 72
 
 
 def taps():
@@ -36,13 +35,13 @@
     return picked * row_ok[:, None] * col_ok[None, :]
 
 
-def stored(tables, edge):
+def stored(tables, edge, axis):
     count = tables.shape[0]
     if count > 2 * edge + 1:
         tables = np.concatenate([tables[: edge + 1], tables[count - edge :]], 0)
     high = tables.astype(np.float32).astype(ml_dtypes.bfloat16)
     low = (tables - high.astype(np.float64)).astype(np.float32).astype(ml_dtypes.bfloat16)
-    return jnp.asarray(np.stack([high, low], 1))
+    return jnp.asarray(np.concatenate([high, low, high] if axis == 2 else [high, high, low], axis))
 
 
 def table_of(index, count, edge):
@@ -69,9 +68,8 @@
         out_ids = np.concatenate(
             [
                 np.arange(start, start + block + 1),
-                off_grid(KEPT - block - 2),
+                off_grid(ROWS - block - 2),
                 [start - 1],
-                off_grid(ROWS - KEPT),
             ]
         )
         in_ids = np.arange(start - 2 * block, start + 3 * block)
@@ -142,8 +140,6 @@
     x_copy.wait()
     centre = float(depth_w[1][0][0])
 
-    x_both = jnp.concatenate([x_ref[0], x_ref[1]], 0)
-    x_high = x_ref[0]
     for pair in range(depth // 2):
         for k in range(2):
             z = 2 * pair + k
@@ -175,66 +171,79 @@
                     slope_ref[2, at, lanes] = 0.5 * (above - below)
         for c, (i, j) in enumerate(((0, 0), (1, 1), (2, 2), (0, 1), (0, 2), (1, 2))):
             high, low = split_f32(slope_ref[i] * slope_ref[j])
-            first = jnp.dot(x_both, high, preferred_element_type=jnp.float32)
-            second = jnp.dot(x_high, low, preferred_element_type=jnp.float32)
-            done = first[: 2 * ROWS] + first[2 * ROWS :] + second
-            fine, coarse = done[:ROWS], done[ROWS:]
-            scale = weight_ref[1, c] * centre
+            done = jnp.dot(
+                x_ref[...],
+                jnp.concatenate([high, high, low], 0),
+                preferred_element_type=jnp.float32,
+            )
+            fine, coarse = done[:ROWS], done[ROWS:] * (weight_ref[1, c] * centre)
+            at = slice((2 * c + pair) * 2 * ROWS, (2 * c + pair + 1) * 2 * ROWS)
+            wide = jnp.concatenate([coarse[:, : 3 * LANES], coarse[:, 3 * LANES :]], 0)
+            high_ref[at, : 3 * LANES], low_ref[at, : 3 * LANES] = split_f32(wide)
             for k in range(2):
                 z = 2 * pair + k
-                at = slice((c * depth + z) * ROWS, (c * depth + z + 1) * ROWS)
-                wide = coarse[:, 3 * k * LANES : 3 * (k + 1) * LANES] * scale
-                high_ref[at, : 3 * LANES], low_ref[at, : 3 * LANES] = split_f32(wide)
                 l, o, r = [
                     fine[:, (3 * k + b) * LANES : (3 * k + b + 1) * LANES] for b in range(3)
                 ]
                 near_ref[c, z, :, :LANES] = o
                 near_ref[c, z, :, LANES:] = jnp.where(lane_index(l.shape) < LANES // 2, r, l)
-    for c in range(6):
-        for z in range(depth):
-            mixed = near_ref[c, 0] * (weight_ref[0, c] * float(depth_w[0][z][0]))
-            for k in range(1, depth):
-                mixed = mixed + near_ref[c, k] * (weight_ref[0, c] * float(depth_w[0][z][k]))
-            at = slice((c * depth + z) * ROWS, (c * depth + z + 1) * ROWS)
-            high_ref[at, 3 * LANES :], low_ref[at, 3 * LANES :] = split_f32(mixed)
     y_copy.wait()
     for c in range(6):
+        planes = [near_ref[c, z] * weight_ref[0, c] for z in range(depth)]
+        for pair in range(depth // 2):
+            mixed = []
+            for z in (2 * pair, 2 * pair + 1):
+                row = [float(w) for w in depth_w[0][z]]
+                mixed.append(sum(planes[k] * row[k] for k in range(1, depth)) + planes[0] * row[0])
+            at = slice((2 * c + pair) * 2 * ROWS, (2 * c + pair + 1) * 2 * ROWS)
+            high_ref[at, 3 * LANES :], low_ref[at, 3 * LANES :] = split_f32(
+                jnp.concatenate(mixed, 0)
+            )
         at = slice(c * depth * ROWS, (c + 1) * depth * ROWS)
         high, low = high_ref[at, :], low_ref[at, :]
-        done = jnp.dot(high, y_ref[0], preferred_element_type=jnp.float32)
-        done = done + jnp.dot(low, y_ref[0], preferred_element_type=jnp.float32)
-        done = done + jnp.dot(high, y_ref[1], preferred_element_type=jnp.float32)
+        done = jnp.dot(
+            jnp.concatenate([high, low, high], 1),
+            y_ref[...],
+            preferred_element_type=jnp.float32,
+        )
         for z in range(depth):
-            out_ref[c, z] = done[z * ROWS : z * ROWS + KEPT]
-
-
-def gradient_kernel(adj_ref, mine_ref, other_ref, own_ref, send_ref):
-    depth, rows, cols = mine_ref.shape
-    block = own_ref.shape[1]
-    for model, result, sign in ((mine_ref, own_ref, 0.5), (other_ref, send_ref, -0.5)):
-        q_z = []
-        total = []
-        for z in range(depth):
-            m = model[z]
-            s_x = 0.5 * (pltpu.roll(m, rows - 1, 0) - pltpu.roll(m, 1, 0))
-            s_y = 0.5 * (pltpu.roll(m, cols - 1, 1) - pltpu.roll(m, 1, 1))
-            above = model[z + 1] if z + 1 < depth else jnp.zeros_like(m)
-            below = model[z - 1] if z > 0 else jnp.zeros_like(m)
-            s_z = 0.5 * (above - below)
-            a = [adj_ref[c, z] for c in range(6)]
-            q_x = 2.0 * a[0] * s_x + a[3] * s_y + a[4] * s_z
-            q_y = 2.0 * a[1] * s_y + a[3] * s_x + a[5] * s_z
-            q_z.append((2.0 * a[2] * s_z + a[4] * s_x + a[5] * s_y)[:block, :LANES])
-            lateral = pltpu.roll(q_x, 1, 0) - pltpu.roll(q_x, rows - 1, 0)
-            lateral = lateral + pltpu.roll(q_y, 1, 1) - pltpu.roll(q_y, cols - 1, 1)
-            total.append(lateral[:block, :LANES])
-        for z in range(depth):
-            value = total[z]
-            if z > 0:
-                value = value + q_z[z - 1]
-            if z + 1 < depth:
-                value = value - q_z[z + 1]
-            result[z] = sign * value
+            out_ref[c, z] = done[z * ROWS : (z + 1) * ROWS]
+
+
+def gradient_kernel(sign, adj_ref, model, result):
+    depth, rows, cols = model.shape
+    block = result.shape[1]
+    q_z = []
+    total = []
+    for z in range(depth):
+        m = model[z]
+        s_x = 0.5 * (pltpu.roll(m, rows - 1, 0) - pltpu.roll(m, 1, 0))
+        s_y = 0.5 * (pltpu.roll(m, cols - 1, 1) - pltpu.roll(m, 1, 1))
+        above = model[z + 1] if z + 1 < depth else jnp.zeros_like(m)
+        below = model[z - 1] if z > 0 else jnp.zeros_like(m)
+        s_z = 0.5 * (above - below)
+        a = [adj_ref[c, z] for c in range(6)]
+        q_x = 2.0 * a[0] * s_x + a[3] * s_y + a[4] * s_z
+        q_y = 2.0 * a[1] * s_y + a[3] * s_x + a[5] * s_z
+        q_z.append((2.0 * a[2] * s_z + a[4] * s_x + a[5] * s_y)[:block, :LANES])
+        lateral = pltpu.roll(q_x, 1, 0) - pltpu.roll(q_x, rows - 1, 0)
+        lateral = lateral + pltpu.roll(q_y, 1, 1) - pltpu.roll(q_y, cols - 1, 1)
+        total.append(lateral[:block, :LANES])
+    for z in range(depth):
+        value = total[z]
+        if z > 0:
+            value = value + q_z[z - 1]
+        if z + 1 < depth:
+            value = value - q_z[z + 1]
+        result[z] = sign * value
+
+
+def swap_columns(value, first):
+    peers = lax.axis_size("gy")
+    route = []
+    for i in range(first, peers - 1, 2):
+        route += [(i, i + 1), (i + 1, i)]
+    return lax.ppermute(value, "gy", route)
 
 
 def shift(value, axis, step):
@@ -251,8 +260,8 @@
         depth, x_cells, y_cells = field.shape
         depth_w = [squared(depth, d).tolist() for d in DILATIONS]
         x_index, y_index = lax.axis_index("gx"), lax.axis_index("gy")
-        x_all = stored(x_tables(x_peers, x_cells), 2)
-        y_all = stored(y_tables(y_peers, y_cells), 1)
+        x_all = stored(x_tables(x_peers, x_cells), 2, 2)
+        y_all = stored(y_tables(y_peers, y_cells), 1, 1)
         which = jnp.stack([x_index, y_index])
         near = [shift(field, "gx", 1), shift(field, "gx", -1)]
         far = [shift(field, "gx", 2), shift(field, "gx", -2)]
@@ -266,7 +275,7 @@
         f32 = jnp.float32
         mine = pl.pallas_call(
             pack_kernel,
-            out_shape=jax.ShapeDtypeStruct((depth, KEPT, 2 * LANES), f32),
+            out_shape=jax.ShapeDtypeStruct((depth, ROWS, 2 * LANES), f32),
             in_specs=[vmem] * 3,
             out_specs=vmem,
             compiler_params=params,
@@ -275,7 +284,7 @@
         rows = 5 * x_cells
         adjoint = pl.pallas_call(
             lambda *refs: smooth_kernel(depth_w, (x_peers, y_peers), *refs),
-            out_shape=jax.ShapeDtypeStruct((6, depth, KEPT, 2 * LANES), f32),
+            out_shape=jax.ShapeDtypeStruct((6, depth, ROWS, 2 * LANES), f32),
             in_specs=[smem] * 2 + [vmem] * 6 + [pl.BlockSpec(memory_space=pl.ANY)] * 2,
             out_specs=vmem,
             scratch_shapes=[
@@ -297,15 +306,20 @@
             which, channel_weight, inner_sides[0], inner, inner_sides[1],
             outer_sides[0], outer, outer_sides[1], x_all, y_all,
         )
-        own, send = pl.pallas_call(
-            gradient_kernel,
-            out_shape=[jax.ShapeDtypeStruct(field.shape, f32)] * 2,
-            in_specs=[vmem] * 3,
-            out_specs=[vmem] * 2,
-            compiler_params=params,
-        )(adjoint, mine, other)
-        got = lax.ppermute(send, "phys", [(0, 1), (1, 0)])
-        return (own + got)[None]
+        def gradient(sign, model):
+            return pl.pallas_call(
+                lambda *refs: gradient_kernel(sign, *refs),
+                out_shape=jax.ShapeDtypeStruct(field.shape, f32),
+                in_specs=[vmem] * 2,
+                out_specs=vmem,
+                compiler_params=params,
+                cost_estimate=pl.CostEstimate(
+                    flops=10**7, bytes_accessed=2 * 10**6, transcendentals=0
+                ),
+            )(adjoint, model)
+
+        got = lax.ppermute(gradient(-0.5, other), "phys", [(0, 1), (1, 0)])
+        return (gradient(0.5, mine) + got)[None]
 
     in_specs = (P("phys", None, "gx", "gy"), P())
     out_specs = P("phys", None, "gx", "gy")

time: 59.2 us -> 56.9 us (0.961)
  Pallas kernels: 10.6 us -> 8.97 us
  waiting for transfers between devices: 13.4 us -> 12.7 us
    pallas_call x1, Pallas kernels: 9.29 us -> 7.64 us  [shards(): pl.pallas_call(lambda *refs: smooth_kernel(depth_w, (x_peers, y_peers), *...]
    ppermute x1, waiting for transfers between devices: 2.42 us -> 1.77 us  [shards(): got = lax.ppermute(gradient(-0.5, other), 'phys', [(0, 1), (1, 0)])]
    pallas_call x2 -> x3, Pallas kernels: 1.29 us -> 1.33 us  [the longest x2 1.3 us: gradient(): pl.pallas_call(lambda *refs: gradient_kernel(sign, *refs), out_shape=jax....]
  transfers between devices with their start and end apart: 10 -> 10, of which waited for: 3 -> 3; matrix products, arithmetic and copies ran while one was open for 2% -> 2% of each run, Pallas kernels for 16% -> 15%
where the time goes in v3:
time: 56.9 us; the launch traced here: 55.9 us
  starting transfers between devices  32.3 us (57%)
  waiting for transfers between devices  12.7 us (22%)
  Pallas kernels  8.97 us (16%)
  other arithmetic  1.68 us (3%)
    ppermute x8, starting transfers between devices, shift(): return lax.ppermute(value, axis, route)  23.2 us
    ppermute x8, waiting for transfers between devices, shift(): return lax.ppermute(value, axis, route)  10.9 us
    pallas_call x1, Pallas kernels, shards(): pl.pallas_call(lambda *refs: smooth_kernel(depth_w, (x_peers, y_peers), *...  7.64 us
    ppermute x1, starting transfers between devices, shards(): got = lax.ppermute(gradient(-0.5, other), 'phys', [(0, 1), (1, 0)])  4.78 us
    ppermute x1, starting transfers between devices, shards(): other = lax.ppermute(mine, 'phys', [(0, 1), (1, 0)])  4.36 us
    ppermute x1, waiting for transfers between devices, shards(): got = lax.ppermute(gradient(-0.5, other), 'phys', [(0, 1), (1, 0)])  1.77 us
    pallas_call x2, Pallas kernels, gradient(): pl.pallas_call(lambda *refs: gradient_kernel(sign, *refs), out_shape=jax....  1.3 us
  transfers between devices with their start and end apart: 10, of which 3 were waited for; matrix products, arithmetic and copies ran while one was open for 2% of the time, Pallas kernels for 15%

profile of v3, /device:TPU:25, one launch (start us, length us, event | category | flops | bytes accessed | tf_op | source)
XLA Modules:
  0.0 55.9 jit_solution(16671403185587859635)
XLA Ops:
  0.0 0.0 copy-start.1
  0.0 0.0 copy-start
  0.0 3.7 %collective-permute-start = (f32[4,64,128]{2,1,0:T(8,128)}, f32[4,64,128]{2,1,0:T(8,128)S(1)}, u32[]{:S(2)}, u32[]{:S(2)}) collective-permute-start(f32[4,64,128]{2,1,0:T(8,128)} %bitcast.5), channel_id=1, source_target_pairs={{0,16},{16,32},{32,48},{48,64},{64,80},{80,96},{96,112},{112,128},... | collective-permute-start | bytes 393224 | tf_op jit(solution)/shard_map/ppermute | solution.py:252
  3.7 1.3 %collective-permute-start.1 = (f32[4,64,128]{2,1,0:T(8,128)}, f32[4,64,128]{2,1,0:T(8,128)S(1)}, u32[]{:S(2)}, u32[]{:S(2)}) collective-permute-start(f32[4,64,128]{2,1,0:T(8,128)} %bitcast.6), channel_id=1, source_target_pairs={{16,0},{32,16},{48,32},{64,48},{80,64},{96,80},{112,96},{128,112},... | collective-permute-start | bytes 393224 | tf_op jit(solution)/shard_map/ppermute | solution.py:252
  5.0 5.5 %collective-permute-start.4 = (f32[4,64,128]{2,1,0:T(8,128)}, f32[4,64,128]{2,1,0:T(8,128)S(1)}, u32[]{:S(2)}, u32[]{:S(2)}) collective-permute-start(f32[4,64,128]{2,1,0:T(8,128)} %bitcast.7), channel_id=1, source_target_pairs={{0,32},{16,48},{32,64},{48,80},{64,96},{80,112},{96,128},{112,144}... | collective-permute-start | bytes 393224 | tf_op jit(solution)/shard_map/ppermute | solution.py:252
  10.5 1.3 %collective-permute-start.5 = (f32[4,64,128]{2,1,0:T(8,128)}, f32[4,64,128]{2,1,0:T(8,128)S(1)}, u32[]{:S(2)}, u32[]{:S(2)}) collective-permute-start(f32[4,64,128]{2,1,0:T(8,128)} %bitcast.8), channel_id=1, source_target_pairs={{32,0},{48,16},{64,32},{80,48},{96,64},{112,80},{128,96},{144,112}... | collective-permute-start | bytes 393224 | tf_op jit(solution)/shard_map/ppermute | solution.py:252
  11.8 0.0 collective-permute-done
  11.8 0.0 collective-permute-done.1
  11.8 0.9 %pad_maximum_fusion.refs_3_.near_ref = f32[4,192,128]{2,1,0:T(8,128)S(1)} fusion(f32[4,64,128]{2,1,0:T(8,128)S(1)} %collective-permute-done.1, f32[4,64,128]{2,1,0:T(8,128)} %bitcast.9, f32[4,64,128]{2,1,0:T(8,128)S(1)} %collective-permute-done), kind=kLoop, calls=%fused_computation | loop fusion | flops 196608 | bytes 786432 | tf_op jit(solution)/shard_map/concatenate | solution.py:268
  12.8 4.0 %collective-permute-start.2 = (f32[4,192,128]{2,1,0:T(8,128)S(1)}, f32[4,192,128]{2,1,0:T(8,128)S(1)}, u32[]{:S(2)}, u32[]{:S(2)}) collective-permute-start(f32[4,192,128]{2,1,0:T(8,128)S(1)} %pad_maximum_fusion.refs_3_.near_ref), channel_id=1, source_target_pairs={{0,1},{1,2},{2,3},{3,4},{4,5},{5,6},{6,7},{7,8},{8,9},{9,10},{10,1... | collective-permute-start | bytes 1179656 | tf_op jit(solution)/shard_map/ppermute | solution.py:252
  16.8 1.9 %collective-permute-start.3 = (f32[4,192,128]{2,1,0:T(8,128)S(1)}, f32[4,192,128]{2,1,0:T(8,128)S(1)}, u32[]{:S(2)}, u32[]{:S(2)}) collective-permute-start(f32[4,192,128]{2,1,0:T(8,128)S(1)} %pad_maximum_fusion.refs_3_.near_ref), channel_id=1, source_target_pairs={{1,0},{2,1},{3,2},{4,3},{5,4},{6,5},{7,6},{8,7},{9,8},{10,9},{11,1... | collective-permute-start | bytes 1179656 | tf_op jit(solution)/shard_map/ppermute | solution.py:252
  18.7 0.0 collective-permute-done.4
  18.7 5.5 %collective-permute-done.5 = f32[4,64,128]{2,1,0:T(8,128)S(1)} collective-permute-done((f32[4,64,128]{2,1,0:T(8,128)}, f32[4,64,128]{2,1,0:T(8,128)S(1)}, u32[]{:S(2)}, u32[]{:S(2)}) %collective-permute-start.5) | collective-permute-done | bytes 131104 | tf_op jit(solution)/shard_map/ppermute | solution.py:252
  24.2 3.6 %collective-permute-start.6 = (f32[4,128,128]{2,1,0:T(8,128)S(1)}, f32[4,128,128]{2,1,0:T(8,128)S(1)}, u32[]{:S(2)}, u32[]{:S(2)}) collective-permute-start(f32[4,128,128]{2,1,0:T(8,128)S(1)} %constant_dynamic-update-slice_fusion.refs_6_), channel_id=1, source_target_pairs={{0,1},{1,2},{2,3},{3,4},{4,5},{5,6},{6,7},{7,8},{8,9},{9,10},{10,1... | collective-permute-start | bytes 786440 | tf_op jit(solution)/shard_map/ppermute | solution.py:252
  27.8 1.9 %collective-permute-start.7 = (f32[4,128,128]{2,1,0:T(8,128)S(1)}, f32[4,128,128]{2,1,0:T(8,128)S(1)}, u32[]{:S(2)}, u32[]{:S(2)}) collective-permute-start(f32[4,128,128]{2,1,0:T(8,128)S(1)} %constant_dynamic-update-slice_fusion.refs_6_), channel_id=1, source_target_pairs={{1,0},{2,1},{3,2},{4,3},{5,4},{6,5},{7,6},{8,7},{9,8},{10,9},{11,1... | collective-permute-start | bytes 786440 | tf_op jit(solution)/shard_map/ppermute | solution.py:252
  29.7 0.1 pad_add_fusion.refs_0_
  29.8 0.0 collective-permute-done.2.refs_2_.left_ref
  29.8 0.0 collective-permute-done.3.refs_4_.right_ref
  29.8 4.4 %collective-permute-start.8 = (f32[4,72,256]{2,1,0:T(8,128)S(1)}, f32[4,72,256]{2,1,0:T(8,128)S(1)}, u32[]{:S(2)}, u32[]{:S(2)}) collective-permute-start(f32[4,72,256]{2,1,0:T(8,128)S(1)} %shard_map.47.refs_1_), channel_id=1, source_target_pairs={{0,256},{256,0},{1,257},{257,1},{2,258},{258,2},{3,259},{259,3},{4... | collective-permute-start | bytes 884744 | tf_op jit(solution)/shard_map/ppermute | solution.py:283
  34.2 0.0 collective-permute-done.6.refs_5_
  34.2 5.4 %collective-permute-done.7.refs_7_ = f32[4,128,128]{2,1,0:T(8,128)S(1)} collective-permute-done((f32[4,128,128]{2,1,0:T(8,128)S(1)}, f32[4,128,128]{2,1,0:T(8,128)S(1)}, u32[]{:S(2)}, u32[]{:S(2)}) %collective-permute-start.7) | collective-permute-done | bytes 262176 | tf_op jit(solution)/shard_map/ppermute | solution.py:252
  39.7 0.0 copy-done.1
  39.7 0.0 copy-done
  39.7 7.6 %shard_map.46.refs_0_ = f32[6,4,72,256]{3,2,1,0:T(8,128)S(1)} custom-call(s32[2]{0:T(128)S(1)} %pad_add_fusion.refs_0_, f32[2,6]{1,0:T(2,128)S(1)} %copy-done, f32[4,192,128]{2,1,0:T(8,128)S(1)} %collective-permute-done.2.refs_2_.left_ref, f32[4,192,128]{2,1,0:T(8,128)S(1)} %pad_maximum_fusion.refs_3_.near_ref, ...), custom_call_target="tpu_custom_call" | custom-call | flops 8000000000 | bytes 4000000 | tf_op jit(solution)/shard_map/pallas_call | solution.py:285
  47.3 0.0 collective-permute-done.8.refs_1_
  47.3 0.7 %shard_map.49 = f32[4,64,128]{2,1,0:T(8,128)S(1)} custom-call(f32[6,4,72,256]{3,2,1,0:T(8,128)S(1)} %shard_map.46.refs_0_, f32[4,72,256]{2,1,0:T(8,128)S(1)} %collective-permute-done.8.refs_1_), custom_call_target="tpu_custom_call" | custom-call | flops 10000000 | bytes 2000000 | tf_op jit(solution)/shard_map/pallas_call | solution.py:310
  48.0 4.8 %collective-permute-start.9 = (f32[4,64,128]{2,1,0:T(8,128)S(1)}, f32[4,64,128]{2,1,0:T(8,128)S(1)}, u32[]{:S(2)}, u32[]{:S(2)}) collective-permute-start(f32[4,64,128]{2,1,0:T(8,128)S(1)} %shard_map.49), channel_id=1, source_target_pairs={{0,256},{256,0},{1,257},{257,1},{2,258},{258,2},{3,259},{259,3},{4... | collective-permute-start | bytes 393224 | tf_op jit(solution)/shard_map/ppermute | solution.py:321
  52.8 0.7 %shard_map.48 = f32[4,64,128]{2,1,0:T(8,128)S(1)} custom-call(f32[6,4,72,256]{3,2,1,0:T(8,128)S(1)} %shard_map.46.refs_0_, f32[4,72,256]{2,1,0:T(8,128)S(1)} %shard_map.47.refs_1_), custom_call_target="tpu_custom_call" | custom-call | flops 10000000 | bytes 2000000 | tf_op jit(solution)/shard_map/pallas_call | solution.py:310
  53.4 1.8 %collective-permute-done.9 = f32[4,64,128]{2,1,0:T(8,128)S(1)} collective-permute-done((f32[4,64,128]{2,1,0:T(8,128)S(1)}, f32[4,64,128]{2,1,0:T(8,128)S(1)}, u32[]{:S(2)}, u32[]{:S(2)}) %collective-permute-start.9) | collective-permute-done | bytes 131104 | tf_op jit(solution)/shard_map/ppermute | solution.py:321
  55.2 0.7 %add_bitcast_fusion = f32[1,4,64,128]{3,2,1,0:T(8,128)} fusion(f32[4,64,128]{2,1,0:T(8,128)S(1)} %shard_map.48, f32[4,64,128]{2,1,0:T(8,128)S(1)} %collective-permute-done.9), kind=kLoop, calls=%fused_computation.1 | loop fusion | flops 32768 | bytes 393216 | tf_op jit(solution)/shard_map/broadcast_in_dim | solution.py:322
  (3 shorter events, 0.0 us)
Async XLA Ops:
  0.0 39.7 %copy-start.1 = (bf16[5,144,960]{2,1,0:T(8,128)(2,1)S(1)}, bf16[5,144,960]{2,1,0:T(8,128)(2,1)}, u32[]{:S(2)}) copy-start(bf16[5,144,960]{2,1,0:T(8,128)(2,1)} %constant.11.clone.refs_8_) | copy-start | bytes 4147204
  0.0 39.7 %copy-start = (f32[2,6]{1,0:T(2,128)S(1)}, f32[2,6]{1,0:T(2,128)}, u32[]{:S(2)}) copy-start(f32[2,6]{1,0:T(2,128)} %refs_1_.1) | copy-start | bytes 148
  0.0 11.8 %collective-permute-start = (f32[4,64,128]{2,1,0:T(8,128)}, f32[4,64,128]{2,1,0:T(8,128)S(1)}, u32[]{:S(2)}, u32[]{:S(2)}) collective-permute-start(f32[4,64,128]{2,1,0:T(8,128)} %bitcast.5), channel_id=1, source_target_pairs={{0,16},{16,32},{32,48},{48,64},{64,80},{80,96},{96,112},{112,128},... | collective-permute-start | bytes 393224 | tf_op jit(solution)/shard_map/ppermute | solution.py:252
  3.7 8.1 %collective-permute-start.1 = (f32[4,64,128]{2,1,0:T(8,128)}, f32[4,64,128]{2,1,0:T(8,128)S(1)}, u32[]{:S(2)}, u32[]{:S(2)}) collective-permute-start(f32[4,64,128]{2,1,0:T(8,128)} %bitcast.6), channel_id=1, source_target_pairs={{16,0},{32,16},{48,32},{64,48},{80,64},{96,80},{112,96},{128,112},... | collective-permute-start | bytes 393224 | tf_op jit(solution)/shard_map/ppermute | solution.py:252
  5.0 13.7 %collective-permute-start.4 = (f32[4,64,128]{2,1,0:T(8,128)}, f32[4,64,128]{2,1,0:T(8,128)S(1)}, u32[]{:S(2)}, u32[]{:S(2)}) collective-permute-start(f32[4,64,128]{2,1,0:T(8,128)} %bitcast.7), channel_id=1, source_target_pairs={{0,32},{16,48},{32,64},{48,80},{64,96},{80,112},{96,128},{112,144}... | collective-permute-start | bytes 393224 | tf_op jit(solution)/shard_map/ppermute | solution.py:252
  10.5 13.7 %collective-permute-start.5 = (f32[4,64,128]{2,1,0:T(8,128)}, f32[4,64,128]{2,1,0:T(8,128)S(1)}, u32[]{:S(2)}, u32[]{:S(2)}) collective-permute-start(f32[4,64,128]{2,1,0:T(8,128)} %bitcast.8), channel_id=1, source_target_pairs={{32,0},{48,16},{64,32},{80,48},{96,64},{112,80},{128,96},{144,112}... | collective-permute-start | bytes 393224 | tf_op jit(solution)/shard_map/ppermute | solution.py:252
  12.8 17.0 %collective-permute-start.2 = (f32[4,192,128]{2,1,0:T(8,128)S(1)}, f32[4,192,128]{2,1,0:T(8,128)S(1)}, u32[]{:S(2)}, u32[]{:S(2)}) collective-permute-start(f32[4,192,128]{2,1,0:T(8,128)S(1)} %pad_maximum_fusion.refs_3_.near_ref), channel_id=1, source_target_pairs={{0,1},{1,2},{2,3},{3,4},{4,5},{5,6},{6,7},{7,8},{8,9},{9,10},{10,1... | collective-permute-start | bytes 1179656 | tf_op jit(solution)/shard_map/ppermute | solution.py:252
  16.8 13.0 %collective-permute-start.3 = (f32[4,192,128]{2,1,0:T(8,128)S(1)}, f32[4,192,128]{2,1,0:T(8,128)S(1)}, u32[]{:S(2)}, u32[]{:S(2)}) collective-permute-start(f32[4,192,128]{2,1,0:T(8,128)S(1)} %pad_maximum_fusion.refs_3_.near_ref), channel_id=1, source_target_pairs={{1,0},{2,1},{3,2},{4,3},{5,4},{6,5},{7,6},{8,7},{9,8},{10,9},{11,1... | collective-permute-start | bytes 1179656 | tf_op jit(solution)/shard_map/ppermute | solution.py:252
  24.2 10.0 %collective-permute-start.6 = (f32[4,128,128]{2,1,0:T(8,128)S(1)}, f32[4,128,128]{2,1,0:T(8,128)S(1)}, u32[]{:S(2)}, u32[]{:S(2)}) collective-permute-start(f32[4,128,128]{2,1,0:T(8,128)S(1)} %constant_dynamic-update-slice_fusion.refs_6_), channel_id=1, source_target_pairs={{0,1},{1,2},{2,3},{3,4},{4,5},{5,6},{6,7},{7,8},{8,9},{9,10},{10,1... | collective-permute-start | bytes 786440 | tf_op jit(solution)/shard_map/ppermute | solution.py:252
  27.8 11.9 %collective-permute-start.7 = (f32[4,128,128]{2,1,0:T(8,128)S(1)}, f32[4,128,128]{2,1,0:T(8,128)S(1)}, u32[]{:S(2)}, u32[]{:S(2)}) collective-permute-start(f32[4,128,128]{2,1,0:T(8,128)S(1)} %constant_dynamic-update-slice_fusion.refs_6_), channel_id=1, source_target_pairs={{1,0},{2,1},{3,2},{4,3},{5,4},{6,5},{7,6},{8,7},{9,8},{10,9},{11,1... | collective-permute-start | bytes 786440 | tf_op jit(solution)/shard_map/ppermute | solution.py:252
  29.8 17.5 %collective-permute-start.8 = (f32[4,72,256]{2,1,0:T(8,128)S(1)}, f32[4,72,256]{2,1,0:T(8,128)S(1)}, u32[]{:S(2)}, u32[]{:S(2)}) collective-permute-start(f32[4,72,256]{2,1,0:T(8,128)S(1)} %shard_map.47.refs_1_), channel_id=1, source_target_pairs={{0,256},{256,0},{1,257},{257,1},{2,258},{258,2},{3,259},{259,3},{4... | collective-permute-start | bytes 884744 | tf_op jit(solution)/shard_map/ppermute | solution.py:283
  48.0 7.2 %collective-permute-start.9 = (f32[4,64,128]{2,1,0:T(8,128)S(1)}, f32[4,64,128]{2,1,0:T(8,128)S(1)}, u32[]{:S(2)}, u32[]{:S(2)}) collective-permute-start(f32[4,64,128]{2,1,0:T(8,128)S(1)} %shard_map.49), channel_id=1, source_target_pairs={{0,256},{256,0},{1,257},{257,1},{2,258},{258,2},{3,259},{259,3},{4... | collective-permute-start | bytes 393224 | tf_op jit(solution)/shard_map/ppermute | solution.py:321

commit v4 on v3

--- a/solution.py
+++ b/solution.py
@@ -318,7 +318,8 @@
                 ),
             )(adjoint, model)
 
-        got = lax.ppermute(gradient(-0.5, other), "phys", [(0, 1), (1, 0)])
+        both = lax.all_gather(gradient(-0.5, other), "phys")
+        got = jnp.where(lax.axis_index("phys") == 0, both[1], both[0])
         return (gradient(0.5, mine) + got)[None]
 
     in_specs = (P("phys", None, "gx", "gy"), P())

time: 56.9 us -> 56.4 us (level)
  blocking collectives: 0 us -> 6 us
  starting transfers between devices: 32.3 us -> 27.5 us
  waiting for transfers between devices: 12.7 us -> 10.9 us
    all_gather x0 -> x1, blocking collectives: none -> 6 us  [shards(): both = lax.all_gather(gradient(-0.5, other), 'phys')]
    ppermute x1 -> x0, starting transfers between devices: 4.78 us -> none  [shards(): got = lax.ppermute(gradient(-0.5, other), 'phys', [(0, 1), (1, 0)])]
    ppermute x1 -> x0, waiting for transfers between devices: 1.77 us -> none  [shards(): got = lax.ppermute(gradient(-0.5, other), 'phys', [(0, 1), (1, 0)])]
  transfers between devices with their start and end apart: 10 -> 9, of which waited for: 3 -> 2; matrix products, arithmetic and copies ran while one was open for 2% -> 2% of each run, Pallas kernels for 15% -> 15%
where the time goes in v4:
time: 56.4 us; the launch traced here: 55.3 us
  starting transfers between devices  27.5 us (49%)
  waiting for transfers between devices  10.9 us (19%)
  Pallas kernels  8.97 us (16%)
  blocking collectives  6 us (11%)
  other arithmetic  1.69 us (3%)
    ppermute x8, starting transfers between devices, shift(): return lax.ppermute(value, axis, route)  23.2 us
    ppermute x8, waiting for transfers between devices, shift(): return lax.ppermute(value, axis, route)  10.9 us
    pallas_call x1, Pallas kernels, shards(): pl.pallas_call(lambda *refs: smooth_kernel(depth_w, (x_peers, y_peers), *...  7.64 us
    all_gather x1, blocking collectives, shards(): both = lax.all_gather(gradient(-0.5, other), 'phys')  6 us
    ppermute x1, starting transfers between devices, shards(): other = lax.ppermute(mine, 'phys', [(0, 1), (1, 0)])  4.36 us
    pallas_call x2, Pallas kernels, gradient(): pl.pallas_call(lambda *refs: gradient_kernel(sign, *refs), out_shape=jax....  1.3 us
  transfers between devices with their start and end apart: 9, of which 2 were waited for; matrix products, arithmetic and copies ran while one was open for 2% of the time, Pallas kernels for 15%

profile of v4, /device:TPU:25, one launch (start us, length us, event | category | flops | bytes accessed | tf_op | source)
XLA Modules:
  0.0 55.3 jit_solution(14183557359438264263)
XLA Ops:
  0.0 0.0 copy-start.1
  0.0 0.0 copy-start
  0.0 3.7 %collective-permute-start = (f32[4,64,128]{2,1,0:T(8,128)}, f32[4,64,128]{2,1,0:T(8,128)S(1)}, u32[]{:S(2)}, u32[]{:S(2)}) collective-permute-start(f32[4,64,128]{2,1,0:T(8,128)} %bitcast.5), channel_id=1, source_target_pairs={{0,16},{16,32},{32,48},{48,64},{64,80},{80,96},{96,112},{112,128},... | collective-permute-start | bytes 393224 | tf_op jit(solution)/shard_map/ppermute | solution.py:252
  3.7 1.3 %collective-permute-start.1 = (f32[4,64,128]{2,1,0:T(8,128)}, f32[4,64,128]{2,1,0:T(8,128)S(1)}, u32[]{:S(2)}, u32[]{:S(2)}) collective-permute-start(f32[4,64,128]{2,1,0:T(8,128)} %bitcast.6), channel_id=1, source_target_pairs={{16,0},{32,16},{48,32},{64,48},{80,64},{96,80},{112,96},{128,112},... | collective-permute-start | bytes 393224 | tf_op jit(solution)/shard_map/ppermute | solution.py:252
  5.0 5.5 %collective-permute-start.4 = (f32[4,64,128]{2,1,0:T(8,128)}, f32[4,64,128]{2,1,0:T(8,128)S(1)}, u32[]{:S(2)}, u32[]{:S(2)}) collective-permute-start(f32[4,64,128]{2,1,0:T(8,128)} %bitcast.7), channel_id=1, source_target_pairs={{0,32},{16,48},{32,64},{48,80},{64,96},{80,112},{96,128},{112,144}... | collective-permute-start | bytes 393224 | tf_op jit(solution)/shard_map/ppermute | solution.py:252
  10.5 1.3 %collective-permute-start.5 = (f32[4,64,128]{2,1,0:T(8,128)}, f32[4,64,128]{2,1,0:T(8,128)S(1)}, u32[]{:S(2)}, u32[]{:S(2)}) collective-permute-start(f32[4,64,128]{2,1,0:T(8,128)} %bitcast.8), channel_id=1, source_target_pairs={{32,0},{48,16},{64,32},{80,48},{96,64},{112,80},{128,96},{144,112}... | collective-permute-start | bytes 393224 | tf_op jit(solution)/shard_map/ppermute | solution.py:252
  11.8 0.0 collective-permute-done
  11.8 0.0 collective-permute-done.1
  11.8 0.9 %pad_maximum_fusion.refs_3_.near_ref = f32[4,192,128]{2,1,0:T(8,128)S(1)} fusion(f32[4,64,128]{2,1,0:T(8,128)S(1)} %collective-permute-done.1, f32[4,64,128]{2,1,0:T(8,128)} %bitcast.9, f32[4,64,128]{2,1,0:T(8,128)S(1)} %collective-permute-done), kind=kLoop, calls=%fused_computation | loop fusion | flops 196608 | bytes 786432 | tf_op jit(solution)/shard_map/concatenate | solution.py:268
  12.8 4.0 %collective-permute-start.2 = (f32[4,192,128]{2,1,0:T(8,128)S(1)}, f32[4,192,128]{2,1,0:T(8,128)S(1)}, u32[]{:S(2)}, u32[]{:S(2)}) collective-permute-start(f32[4,192,128]{2,1,0:T(8,128)S(1)} %pad_maximum_fusion.refs_3_.near_ref), channel_id=1, source_target_pairs={{0,1},{1,2},{2,3},{3,4},{4,5},{5,6},{6,7},{7,8},{8,9},{9,10},{10,1... | collective-permute-start | bytes 1179656 | tf_op jit(solution)/shard_map/ppermute | solution.py:252
  16.8 1.9 %collective-permute-start.3 = (f32[4,192,128]{2,1,0:T(8,128)S(1)}, f32[4,192,128]{2,1,0:T(8,128)S(1)}, u32[]{:S(2)}, u32[]{:S(2)}) collective-permute-start(f32[4,192,128]{2,1,0:T(8,128)S(1)} %pad_maximum_fusion.refs_3_.near_ref), channel_id=1, source_target_pairs={{1,0},{2,1},{3,2},{4,3},{5,4},{6,5},{7,6},{8,7},{9,8},{10,9},{11,1... | collective-permute-start | bytes 1179656 | tf_op jit(solution)/shard_map/ppermute | solution.py:252
  18.7 0.0 collective-permute-done.4
  18.7 5.5 %collective-permute-done.5 = f32[4,64,128]{2,1,0:T(8,128)S(1)} collective-permute-done((f32[4,64,128]{2,1,0:T(8,128)}, f32[4,64,128]{2,1,0:T(8,128)S(1)}, u32[]{:S(2)}, u32[]{:S(2)}) %collective-permute-start.5) | collective-permute-done | bytes 131104 | tf_op jit(solution)/shard_map/ppermute | solution.py:252
  24.2 3.6 %collective-permute-start.6 = (f32[4,128,128]{2,1,0:T(8,128)S(1)}, f32[4,128,128]{2,1,0:T(8,128)S(1)}, u32[]{:S(2)}, u32[]{:S(2)}) collective-permute-start(f32[4,128,128]{2,1,0:T(8,128)S(1)} %constant_dynamic-update-slice_fusion.refs_6_), channel_id=1, source_target_pairs={{0,1},{1,2},{2,3},{3,4},{4,5},{5,6},{6,7},{7,8},{8,9},{9,10},{10,1... | collective-permute-start | bytes 786440 | tf_op jit(solution)/shard_map/ppermute | solution.py:252
  27.8 1.9 %collective-permute-start.7 = (f32[4,128,128]{2,1,0:T(8,128)S(1)}, f32[4,128,128]{2,1,0:T(8,128)S(1)}, u32[]{:S(2)}, u32[]{:S(2)}) collective-permute-start(f32[4,128,128]{2,1,0:T(8,128)S(1)} %constant_dynamic-update-slice_fusion.refs_6_), channel_id=1, source_target_pairs={{1,0},{2,1},{3,2},{4,3},{5,4},{6,5},{7,6},{8,7},{9,8},{10,9},{11,1... | collective-permute-start | bytes 786440 | tf_op jit(solution)/shard_map/ppermute | solution.py:252
  29.7 0.1 pad_add_fusion.refs_0_
  29.8 0.0 collective-permute-done.2.refs_2_.left_ref
  29.8 0.0 collective-permute-done.3.refs_4_.right_ref
  29.9 4.4 %collective-permute-start.8 = (f32[4,72,256]{2,1,0:T(8,128)S(1)}, f32[4,72,256]{2,1,0:T(8,128)S(1)}, u32[]{:S(2)}, u32[]{:S(2)}) collective-permute-start(f32[4,72,256]{2,1,0:T(8,128)S(1)} %shard_map.47.refs_1_), channel_id=1, source_target_pairs={{0,256},{256,0},{1,257},{257,1},{2,258},{258,2},{3,259},{259,3},{4... | collective-permute-start | bytes 884744 | tf_op jit(solution)/shard_map/ppermute | solution.py:283
  34.2 0.0 collective-permute-done.6.refs_5_
  34.2 5.4 %collective-permute-done.7.refs_7_ = f32[4,128,128]{2,1,0:T(8,128)S(1)} collective-permute-done((f32[4,128,128]{2,1,0:T(8,128)S(1)}, f32[4,128,128]{2,1,0:T(8,128)S(1)}, u32[]{:S(2)}, u32[]{:S(2)}) %collective-permute-start.7) | collective-permute-done | bytes 262176 | tf_op jit(solution)/shard_map/ppermute | solution.py:252
  39.6 0.0 copy-done.1
  39.7 0.0 copy-done
  39.7 7.6 %shard_map.46.refs_0_ = f32[6,4,72,256]{3,2,1,0:T(8,128)S(1)} custom-call(s32[2]{0:T(128)S(1)} %pad_add_fusion.refs_0_, f32[2,6]{1,0:T(2,128)S(1)} %copy-done, f32[4,192,128]{2,1,0:T(8,128)S(1)} %collective-permute-done.2.refs_2_.left_ref, f32[4,192,128]{2,1,0:T(8,128)S(1)} %pad_maximum_fusion.refs_3_.near_ref, ...), custom_call_target="tpu_custom_call" | custom-call | flops 8000000000 | bytes 4000000 | tf_op jit(solution)/shard_map/pallas_call | solution.py:285
  47.3 0.7 %shard_map.48 = f32[4,64,128]{2,1,0:T(8,128)S(1)} custom-call(f32[6,4,72,256]{3,2,1,0:T(8,128)S(1)} %shard_map.46.refs_0_, f32[4,72,256]{2,1,0:T(8,128)S(1)} %shard_map.47.refs_1_), custom_call_target="tpu_custom_call" | custom-call | flops 10000000 | bytes 2000000 | tf_op jit(solution)/shard_map/pallas_call | solution.py:310
  48.0 0.0 collective-permute-done.8.refs_1_
  48.0 0.7 %shard_map.49 = f32[4,64,128]{2,1,0:T(8,128)S(1)} custom-call(f32[6,4,72,256]{3,2,1,0:T(8,128)S(1)} %shard_map.46.refs_0_, f32[4,72,256]{2,1,0:T(8,128)S(1)} %collective-permute-done.8.refs_1_), custom_call_target="tpu_custom_call" | custom-call | flops 10000000 | bytes 2000000 | tf_op jit(solution)/shard_map/pallas_call | solution.py:310
  48.6 6.0 %all-gather = f32[8,64,128]{2,1,0:T(8,128)S(1)} all-gather(f32[4,64,128]{2,1,0:T(8,128)S(1)} %shard_map.49), channel_id=2, replica_groups=mesh['phys'=2,'gx'=16,'gy'=16] {'phys'}, dimensions={0}, use_global_device_ids=true | all-gather | bytes 393216 | tf_op jit(solution)/shard_map/all_gather | solution.py:321
  54.6 0.7 %fusion.1 = f32[1,4,64,128]{3,2,1,0:T(8,128)} fusion(f32[4,64,128]{2,1,0:T(8,128)S(1)} %shard_map.48, f32[8,64,128]{2,1,0:T(8,128)S(1)} %all-gather, pred[]{:T(512)S(6)} %eq.3), kind=kLoop, calls=%fused_computation.3 | loop fusion | flops 65536 | bytes 524289 | tf_op jit(solution)/shard_map/broadcast_in_dim | solution.py:323
  (3 shorter events, 0.0 us)
Async XLA Ops:
  0.0 39.6 %copy-start.1 = (bf16[5,144,960]{2,1,0:T(8,128)(2,1)S(1)}, bf16[5,144,960]{2,1,0:T(8,128)(2,1)}, u32[]{:S(2)}) copy-start(bf16[5,144,960]{2,1,0:T(8,128)(2,1)} %constant.19.clone.refs_8_) | copy-start | bytes 4147204
  0.0 39.7 %copy-start = (f32[2,6]{1,0:T(2,128)S(1)}, f32[2,6]{1,0:T(2,128)}, u32[]{:S(2)}) copy-start(f32[2,6]{1,0:T(2,128)} %refs_1_.1) | copy-start | bytes 148
  0.0 11.8 %collective-permute-start = (f32[4,64,128]{2,1,0:T(8,128)}, f32[4,64,128]{2,1,0:T(8,128)S(1)}, u32[]{:S(2)}, u32[]{:S(2)}) collective-permute-start(f32[4,64,128]{2,1,0:T(8,128)} %bitcast.5), channel_id=1, source_target_pairs={{0,16},{16,32},{32,48},{48,64},{64,80},{80,96},{96,112},{112,128},... | collective-permute-start | bytes 393224 | tf_op jit(solution)/shard_map/ppermute | solution.py:252
  3.7 8.1 %collective-permute-start.1 = (f32[4,64,128]{2,1,0:T(8,128)}, f32[4,64,128]{2,1,0:T(8,128)S(1)}, u32[]{:S(2)}, u32[]{:S(2)}) collective-permute-start(f32[4,64,128]{2,1,0:T(8,128)} %bitcast.6), channel_id=1, source_target_pairs={{16,0},{32,16},{48,32},{64,48},{80,64},{96,80},{112,96},{128,112},... | collective-permute-start | bytes 393224 | tf_op jit(solution)/shard_map/ppermute | solution.py:252
  5.0 13.7 %collective-permute-start.4 = (f32[4,64,128]{2,1,0:T(8,128)}, f32[4,64,128]{2,1,0:T(8,128)S(1)}, u32[]{:S(2)}, u32[]{:S(2)}) collective-permute-start(f32[4,64,128]{2,1,0:T(8,128)} %bitcast.7), channel_id=1, source_target_pairs={{0,32},{16,48},{32,64},{48,80},{64,96},{80,112},{96,128},{112,144}... | collective-permute-start | bytes 393224 | tf_op jit(solution)/shard_map/ppermute | solution.py:252
  10.5 13.7 %collective-permute-start.5 = (f32[4,64,128]{2,1,0:T(8,128)}, f32[4,64,128]{2,1,0:T(8,128)S(1)}, u32[]{:S(2)}, u32[]{:S(2)}) collective-permute-start(f32[4,64,128]{2,1,0:T(8,128)} %bitcast.8), channel_id=1, source_target_pairs={{32,0},{48,16},{64,32},{80,48},{96,64},{112,80},{128,96},{144,112}... | collective-permute-start | bytes 393224 | tf_op jit(solution)/shard_map/ppermute | solution.py:252
  12.8 17.0 %collective-permute-start.2 = (f32[4,192,128]{2,1,0:T(8,128)S(1)}, f32[4,192,128]{2,1,0:T(8,128)S(1)}, u32[]{:S(2)}, u32[]{:S(2)}) collective-permute-start(f32[4,192,128]{2,1,0:T(8,128)S(1)} %pad_maximum_fusion.refs_3_.near_ref), channel_id=1, source_target_pairs={{0,1},{1,2},{2,3},{3,4},{4,5},{5,6},{6,7},{7,8},{8,9},{9,10},{10,1... | collective-permute-start | bytes 1179656 | tf_op jit(solution)/shard_map/ppermute | solution.py:252
  16.8 13.0 %collective-permute-start.3 = (f32[4,192,128]{2,1,0:T(8,128)S(1)}, f32[4,192,128]{2,1,0:T(8,128)S(1)}, u32[]{:S(2)}, u32[]{:S(2)}) collective-permute-start(f32[4,192,128]{2,1,0:T(8,128)S(1)} %pad_maximum_fusion.refs_3_.near_ref), channel_id=1, source_target_pairs={{1,0},{2,1},{3,2},{4,3},{5,4},{6,5},{7,6},{8,7},{9,8},{10,9},{11,1... | collective-permute-start | bytes 1179656 | tf_op jit(solution)/shard_map/ppermute | solution.py:252
  24.2 10.0 %collective-permute-start.6 = (f32[4,128,128]{2,1,0:T(8,128)S(1)}, f32[4,128,128]{2,1,0:T(8,128)S(1)}, u32[]{:S(2)}, u32[]{:S(2)}) collective-permute-start(f32[4,128,128]{2,1,0:T(8,128)S(1)} %constant_dynamic-update-slice_fusion.refs_6_), channel_id=1, source_target_pairs={{0,1},{1,2},{2,3},{3,4},{4,5},{5,6},{6,7},{7,8},{8,9},{9,10},{10,1... | collective-permute-start | bytes 786440 | tf_op jit(solution)/shard_map/ppermute | solution.py:252
  27.8 11.9 %collective-permute-start.7 = (f32[4,128,128]{2,1,0:T(8,128)S(1)}, f32[4,128,128]{2,1,0:T(8,128)S(1)}, u32[]{:S(2)}, u32[]{:S(2)}) collective-permute-start(f32[4,128,128]{2,1,0:T(8,128)S(1)} %constant_dynamic-update-slice_fusion.refs_6_), channel_id=1, source_target_pairs={{1,0},{2,1},{3,2},{4,3},{5,4},{6,5},{7,6},{8,7},{9,8},{10,9},{11,1... | collective-permute-start | bytes 786440 | tf_op jit(solution)/shard_map/ppermute | solution.py:252
  29.9 18.1 %collective-permute-start.8 = (f32[4,72,256]{2,1,0:T(8,128)S(1)}, f32[4,72,256]{2,1,0:T(8,128)S(1)}, u32[]{:S(2)}, u32[]{:S(2)}) collective-permute-start(f32[4,72,256]{2,1,0:T(8,128)S(1)} %shard_map.47.refs_1_), channel_id=1, source_target_pairs={{0,256},{256,0},{1,257},{257,1},{2,258},{258,2},{3,259},{259,3},{4... | collective-permute-start | bytes 884744 | tf_op jit(solution)/shard_map/ppermute | solution.py:283
